TPU v7x, 256 devices: a whole 4x4x8 slice. The times are simulated.
256 devices in a mesh: section: 8 (over z_lo, core), dp: 32 (over z_hi, x, y).
Axes of the slice: x: 4, y: 4, z: 8 (z_hi: 2, z_lo: 4; z = z_hi * 4 + z_lo), core: 2. Of those that a mesh axis runs over, the one named last changes fastest.
Arguments:
- inflow: bfloat16 [8, 4096, 7168], P('section', 'dp'), may hold values from -6 to 6
- entering: bfloat16 [1, 4096, 7168], P(None, 'dp'), may hold values from -6 to 6
- arrive_grad: bfloat16 [8, 4096, 7168], P('section', 'dp'), may hold values from -12 to 12
- enter_grad: bfloat16 [1, 4096, 7168], P(None, 'dp'), may hold values from -6 to 6
- stashed: bfloat16 [8, 4096, 7168], P('section', 'dp'), may hold values from -12 to 12
- w_down: bfloat16 [8, 7168, 256], P('section', 'dp'), may hold values from -0.0625 to 0.0625
- w_up: bfloat16 [8, 256, 7168], P('section', None, 'dp'), may hold values from -0.375 to 0.375
- norm_gain: float32 [8, 7168], P('section'), may hold values from 0.25 to 1.75
- latent_gain: float32 [8, 256], P('section'), may hold values from 0.25 to 1.75
Outputs:
- leaving_acts: bfloat16 [8, 4096, 7168], P('section', 'dp')
- leaving_grads: bfloat16 [8, 4096, 7168], P('section', 'dp')
- grad_down: float32 [8, 7168, 256], P('section', 'dp')
- grad_up: float32 [8, 256, 7168], P('section', None, 'dp')
- grad_norm_gain: float32 [8, 7168], P('section', 'dp')
- grad_latent_gain: float32 [8, 256], P('section', 'dp')
All inputs are finite; a program needn't handle non-finite values.
Results may differ from a plain program's by a relative error of at most 0.0062.
Values may be sent and summed in bfloat16 or wider, within the bound.
A program may use at most 128 MiB of HBM per device.

v0:
```python
import jax
import jax.numpy as jnp
from jax import lax
from jax.sharding import PartitionSpec as P

epsilon = 1e-06


def passed_along(value, axis, steps):
    count = lax.axis_size(axis)
    first, last = (max(0, -steps), min(count, count - steps))
    return lax.ppermute(value, axis, [(source, source + steps) for source in range(first, last)])


def forward_block(rows_in, down, upward, gain_in, gain_lat):
    wide_in = rows_in.astype(jnp.float32)
    in_scale = lax.rsqrt(jnp.mean(wide_in * wide_in, axis=-1, keepdims=True) + epsilon)
    normed = (wide_in * in_scale * gain_in).astype(jnp.bfloat16)
    latent = jnp.dot(normed, down, preferred_element_type=jnp.float32)
    lat_scale = lax.rsqrt(jnp.mean(latent * latent, axis=-1, keepdims=True) + epsilon)
    lat_norm = latent * lat_scale
    lat_out = (lat_norm * gain_lat).astype(jnp.bfloat16)
    result = (wide_in + jnp.dot(lat_out, upward, preferred_element_type=jnp.float32)).astype(
        jnp.bfloat16
    )
    return (result, (wide_in, in_scale, normed, lat_norm, lat_scale, lat_out))


def backward_saved(saved, grad_rows, down, upward, gain_in, gain_lat):
    wide_in, in_scale, normed, lat_norm, lat_scale, lat_out = saved
    grad_lat = jnp.dot(grad_rows, upward.T, preferred_element_type=jnp.float32)
    grad_upward = jnp.dot(lat_out.T, grad_rows, preferred_element_type=jnp.float32)
    grad_glat = jnp.sum(grad_lat * lat_norm, axis=0)
    grad_norm = grad_lat * gain_lat
    grad_raw = lat_scale * (
        grad_norm - lat_norm * jnp.mean(grad_norm * lat_norm, axis=-1, keepdims=True)
    )
    grad_half = grad_raw.astype(jnp.bfloat16)
    grad_normed = jnp.dot(grad_half, down.T, preferred_element_type=jnp.float32)
    grad_downward = jnp.dot(normed.T, grad_half, preferred_element_type=jnp.float32)
    in_norm = wide_in * in_scale
    grad_gin = jnp.sum(grad_normed * in_norm, axis=0)
    grad_in = grad_normed * gain_in
    grad_back = (
        grad_rows.astype(jnp.float32)
        + in_scale * (grad_in - in_norm * jnp.mean(grad_in * in_norm, axis=-1, keepdims=True))
    ).astype(jnp.bfloat16)
    return (grad_back, grad_downward, grad_upward, grad_gin, grad_glat)


def on_device(
    inflow, entering, arrive_grad, enter_grad, stashed, w_down, w_up, norm_gain, latent_gain
):
    section_pos = lax.axis_index("section")
    section_count = lax.axis_size("section")
    is_first = section_pos == 0
    is_last = section_pos == section_count - 1
    full_down, full_up = (
        lax.all_gather(w_down, "dp", axis=1, tiled=True),
        lax.all_gather(w_up, "dp", axis=2, tiled=True),
    )
    down = full_down[0]
    upward = full_up[0]
    gain_in = norm_gain[0]
    gain_lat = latent_gain[0]
    tick_total = entering.shape[0] + 1
    acts_now = inflow[0]
    grads_now = arrive_grad[0]
    stored = stashed[0]
    totals = None
    for tick_id in range(tick_total):
        result, saved = forward_block(acts_now, down, upward, gain_in, gain_lat)
        _, earlier = forward_block(stored, down, upward, gain_in, gain_lat)
        grad_back, g_down, g_up, g_gin, g_glat = backward_saved(
            earlier, grads_now, down, upward, gain_in, gain_lat
        )
        terms = (g_down, g_up, g_gin, g_glat)
        if totals is None:
            totals = terms
        else:
            totals = tuple((left + right for left, right in zip(totals, terms)))
        stored = acts_now
        if tick_id < tick_total - 1:
            moved_acts = passed_along(result, "section", 1)
            moved_grads = passed_along(grad_back, "section", -1)
            acts_now = jnp.where(is_first, entering[tick_id], moved_acts)
            grads_now = jnp.where(is_last, enter_grad[tick_id], moved_grads)
    shares = (
        lax.psum_scatter(totals[0], "dp", scatter_dimension=0, tiled=True),
        lax.psum_scatter(totals[1], "dp", scatter_dimension=1, tiled=True),
        lax.psum_scatter(totals[2], "dp", scatter_dimension=0, tiled=True),
        lax.psum_scatter(totals[3], "dp", scatter_dimension=0, tiled=True),
    )
    return (
        result[None],
        grad_back[None],
        shares[0][None],
        shares[1][None],
        shares[2][None],
        shares[3][None],
    )


def solution(mesh):
    in_specs = (
        P("section", "dp", None),
        P(None, "dp", None),
        P("section", "dp", None),
        P(None, "dp", None),
        P("section", "dp", None),
        P("section", "dp", None),
        P("section", None, "dp"),
        P("section", None),
        P("section", None),
    )
    out_specs = (
        P("section", "dp", None),
        P("section", "dp", None),
        P("section", "dp", None),
        P("section", None, "dp"),
        P("section", "dp"),
        P("section", "dp"),
    )
    return jax.shard_map(
        on_device, mesh=mesh, in_specs=in_specs, out_specs=out_specs, check_vma=False
    )
```

profile of v0, /device:TPU:1, one launch (start us, length us, event | category | flops | bytes accessed | tf_op | source)
XLA Modules:
  0.0 815.8 jit_solution(5140736122262425549)
XLA Ops:
  7.2 0.0 all-gather.3.cloned.1.call-start
  7.2 0.7 all-gather.3.cloned.1.call-update
  7.9 0.0 all-gather.5.cloned.1.call-start
  7.9 0.7 all-gather.5.cloned.1.call-update
  8.6 0.0 reduce-scatter.3.cloned.1.call-start
  8.7 1.9 fusion.32
  10.6 0.0 copy-start.15
  10.7 110.0 %all-gather.3.cloned.1.call-done = bf16[1,7168,256]{2,1,0:T(8,128)(2,1)} async-done(((bf16[1,224,256]{2,1,0:T(8,128)(2,1)}), bf16[1,7168,256]{2,1,0:T(8,128)(2,1)}) %all-gather.3.cloned.1.call-update) | async-done | bytes 3670032 | tf_op jit(solution)/shard_map/all_gather | solution.py:59
  120.6 3.4 multiply_reduce_fusion.4
  124.0 0.0 copy-start.3
  124.0 0.0 copy-start.14
  124.1 100.8 %all-gather.5.cloned.1.call-done = bf16[1,256,7168]{1,2,0:T(8,128)(2,1)} async-done(((bf16[1,256,224]{1,2,0:T(8,128)(2,1)}), bf16[1,256,7168]{1,2,0:T(8,128)(2,1)}) %all-gather.5.cloned.1.call-update) | async-done | bytes 3670032 | tf_op jit(solution)/shard_map/all_gather | solution.py:60
  224.8 0.0 copy-done.15
  224.8 3.5 multiply_reduce_fusion.1
  228.3 0.1 multiply_convert_fusion.2
  228.4 0.0 copy-done.3
  228.4 0.0 copy-done.14
  228.5 0.1 copy-done.11
  228.5 1.5 fusion.31
  230.0 0.0 copy-done.4
  230.0 0.5 copy-done.9
  230.6 2.4 fusion.29
  233.0 4.2 collective-permute-start.1
  237.2 0.0 copy-done.2
  237.2 0.4 fusion.22
  237.7 0.0 copy-start.5
  237.7 2.9 multiply_reduce_fusion.6
  240.6 0.0 copy-done.5
  240.6 0.0 copy-start.13
  240.6 1.2 fusion.57
  241.9 0.0 copy-start
  241.9 16.6 %collective-permute-done.1 = bf16[128,7168]{1,0:T(8,128)(2,1)} collective-permute-done((bf16[128,7168]{1,0:T(8,128)(2,1)}, bf16[128,7168]{1,0:T(8,128)(2,1)}, u32[]{:S(2)}, u32[]{:S(2)}) %collective-permute-start.1) | collective-permute-done | bytes 1835040 | tf_op jit(solution)/shard_map/ppermute | solution.py:12
  258.5 0.0 copy-done.13
  258.5 1.7 bitcast_select_fusion
  260.2 0.0 copy-start.6
  260.2 0.0 copy-done
  260.3 0.8 multiply_reduce_fusion
  261.0 0.5 copy-done.6
  261.5 0.1 multiply_convert_fusion.1
  261.6 4.3 convolution_add_fusion.1
  265.9 0.0 reduce-scatter.3.cloned.1.call-update
  266.0 0.2 reduce-scatter.5.cloned.1.call-start
  266.2 0.0 copy-start.7
  266.2 2.8 fusion.63
  269.0 0.0 copy-done.7
  269.0 4.2 convolution_add_fusion
  273.3 0.0 reduce-scatter.5.cloned.1.call-update
  273.3 0.0 copy-start.16
  273.3 4.6 fusion
  277.9 1.9 collective-permute-start
  279.8 0.0 copy-done.16
  279.8 0.6 dynamic-slice
  281.7 5.3 fusion.21
  287.1 240.2 %all-reduce.2 = (f32[7168]{0:T(1024)S(1)}, f32[256]{0:T(256)S(1)}) all-reduce(f32[7168]{0:T(1024)S(1)} %add.94, f32[256]{0:T(256)S(1)} %add.95), channel_id=4, replica_groups=mesh['section'=8,'dp'=32] {'dp'}, use_global_device_ids=true, to_apply=%region_14.15.clone | all-reduce | flops 7424 | bytes 59392
  527.3 0.6 dynamic-slice.1
  527.9 0.6 dynamic-slice_bitcast_fusion
  528.5 0.0 collective-permute-done
  528.5 2.8 fusion.35
  531.3 0.8 multiply_reduce_fusion.5
  532.1 1.2 copy-done.1
  533.3 2.5 fusion.2
  535.9 0.7 copy-done.10
  536.6 2.4 fusion.62
  538.9 270.3 %reduce-scatter.5.cloned.1.call-done = f32[256,224]{0,1:T(8,128)} async-done(((f32[256,7168]{0,1:T(8,128)}), f32[256,224]{0,1:T(8,128)}) %reduce-scatter.5.cloned.1.call-update) | async-done | bytes 229392 | tf_op jit(solution)/shard_map/reduce_scatter | solution.py:90
  (23 shorter events, 0.1 us)
Async XLA Ops:
  7.2 113.5 %all-gather.3.cloned.1.call-start = ((), (), s32[]{:S(2)}) async-start(), calls=%async_computation.2 | async-start | bytes 3784704 | tf_op jit(solution)/shard_map/all_gather | solution.py:59
  7.9 216.9 %all-gather.5.cloned.1.call-start = ((), (), s32[]{:S(2)}) async-start(), calls=%async_computation.3 | async-start | bytes 3784704 | tf_op jit(solution)/shard_map/all_gather | solution.py:60
  8.6 530.3 %reduce-scatter.3.cloned.1.call-start = ((), (), s32[]{:S(2)}) async-start(), calls=%async_computation.4 | async-start | bytes 7569408 | tf_op jit(solution)/shard_map/reduce_scatter | solution.py:89
  10.6 214.2 %copy-start.15 = (f32[1,256]{1,0:T(1,128)S(1)}, f32[1,256]{1,0:T(1,128)}, u32[]{:S(2)}) copy-start(f32[1,256]{1,0:T(1,128)} %param.17) | copy-start | bytes 3076
  124.0 104.4 %copy-start.3 = (bf16[1,128,7168]{2,1,0:T(8,128)(2,1)S(1)}, bf16[1,128,7168]{2,1,0:T(8,128)(2,1)}, u32[]{:S(2)}) copy-start(bf16[1,128,7168]{2,1,0:T(8,128)(2,1)} %param.13) | copy-start | bytes 5505028
  124.0 104.4 %copy-start.14 = (f32[1,7168]{1,0:T(1,128)S(1)}, f32[1,7168]{1,0:T(1,128)}, u32[]{:S(2)}) copy-start(f32[1,7168]{1,0:T(1,128)} %param.16) | copy-start | bytes 86020
  224.8 3.7 copy-start.11
  228.5 1.5 copy-start.4
  228.5 2.0 copy-start.9
  230.6 6.6 copy-start.2
  233.0 25.6 %collective-permute-start.1 = (bf16[128,7168]{1,0:T(8,128)(2,1)}, bf16[128,7168]{1,0:T(8,128)(2,1)}, u32[]{:S(2)}, u32[]{:S(2)}) collective-permute-start(bf16[128,7168]{1,0:T(8,128)(2,1)} %fusion.29), channel_id=1, source_target_pairs={{32,0},{64,32},{96,64},{128,96},{160,128},{192,160},{224,192},{33,... | collective-permute-start | bytes 5505032 | tf_op jit(solution)/shard_map/ppermute | solution.py:12
  237.7 3.0 copy-start.5
  240.6 17.9 %copy-start.13 = (bf16[1,128,7168]{2,1,0:T(8,128)(2,1)S(1)}, bf16[1,128,7168]{2,1,0:T(8,128)(2,1)}, u32[]{:S(2)}) copy-start(bf16[1,128,7168]{2,1,0:T(8,128)(2,1)} %param.12) | copy-start | bytes 5505028
  241.9 18.4 %copy-start = (bf16[1,256,7168]{1,2,0:T(8,128)(2,1)S(1)}, bf16[1,256,7168]{1,2,0:T(8,128)(2,1)}, u32[]{:S(2)}) copy-start(bf16[1,256,7168]{1,2,0:T(8,128)(2,1)} %all-gather.5.cloned.1.call-done) | copy-start | bytes 11010052
  260.2 1.3 copy-start.6
  266.0 543.3 %reduce-scatter.5.cloned.1.call-start = ((), (), s32[]{:S(2)}) async-start(), calls=%async_computation.5 | async-start | bytes 7569408 | tf_op jit(solution)/shard_map/reduce_scatter | solution.py:90
  266.2 2.8 copy-start.7
  273.3 6.5 copy-start.16
  277.9 250.6 %collective-permute-start = (bf16[128,7168]{1,0:T(8,128)(2,1)}, bf16[128,7168]{1,0:T(8,128)(2,1)}, u32[]{:S(2)}, u32[]{:S(2)}) collective-permute-start(bf16[128,7168]{1,0:T(8,128)(2,1)} %fusion), channel_id=1, source_target_pairs={{0,32},{32,64},{64,96},{96,128},{128,160},{160,192},{192,224},{1,3... | collective-permute-start | bytes 5505032 | tf_op jit(solution)/shard_map/ppermute | solution.py:12
  527.3 4.0 copy-start.12
  531.3 2.0 copy-start.1
  533.3 2.6 copy-start.8
  533.3 3.3 copy-start.10
Sparse Core Ops, SparseCore 0:
  11.4 109.1 all-gather.2
  124.1 100.7 all-gather.4
  266.1 241.5 reduce-scatter.2
  510.6 298.5 reduce-scatter.4
where the time goes:
time: 832 us; the launch traced here: 816 us
  waiting for transfers between devices  499 us (60%)
  blocking collectives  240 us (29%)
  matrix products  37.9 us (5%)
  between operations  15.3 us (2%)
  other arithmetic  11.9 us (1%)
    reduce_scatter x1, waiting for transfers between devices, on_device(): lax.psum_scatter(totals[1], 'dp', scatter_dimension=1, tiled=True)  270 us
    unnamed x1, blocking collectives  240 us
    all_gather x1, waiting for transfers between devices, on_device(): lax.all_gather(w_down, 'dp', axis=1, tiled=True)  110 us
    all_gather x1, waiting for transfers between devices, on_device(): lax.all_gather(w_up, 'dp', axis=2, tiled=True)  101 us
  transfers between devices with their start and end apart: 6, of which 4 were waited for; matrix products, arithmetic and copies ran while one was open for 5% of the time, Pallas kernels for 0%

commit v1 on v0

v1 whole, which is shorter than its diff:
```python
import functools

import jax
import jax.numpy as jnp
from jax import lax
from jax.experimental import pallas as pl
from jax.experimental.pallas import tpu as pltpu
from jax.sharding import PartitionSpec as P

EPS = 1e-06
MESH = pl.DeviceIdType.MESH
F32 = jnp.float32
BF16 = jnp.bfloat16

D = 7168
R = 256
T = 128
UNIT = 224
HALF = 112
NEAR = 64
FAR = HALF - NEAR
ROW = 4 * UNIT
ROWS = D // ROW


def nt(a, b):
    return lax.dot_general(a, b, (((1,), (1,)), ((), ())), preferred_element_type=F32)


def tn(a, b):
    return lax.dot_general(a, b, (((0,), (0,)), ((), ())), preferred_element_type=F32)


def nn(a, b):
    return jnp.dot(a, b, preferred_element_type=F32)


def kernel(
    inflow, entering, arrive, enter, stashed, wd_in, wu_in, gin, glat,
    out_act, out_grad, out_down, out_up, out_lg,
    W, G, X, N, GG, A1, N1, R0, B0, OA, OB,
    land4, land2, landn, landf, land1, landz,
    LAT, LN, LS, LO, GL, RAW, MT, SC, LGP, LGL,
    gsend, grecv, zsend, zrecv, rsend, rrecv, asend, arecv, bsend, brecv,
    lsend, lrecv, isem, osem,
):
    s = lax.axis_index("section")
    d = lax.axis_index("dp")
    zh = d // 16
    x = (d // 4) % 4
    y = d % 4
    other = 1 - zh
    not_last = s < 7
    not_first = s > 0

    def dp_of(zz, xx, yy):
        return zz * 16 + xx * 4 + yy

    def along(axis, k):
        if axis == 0:
            return (s, dp_of(zh, (x + k) % 4, y))
        return (s, dp_of(zh, x, (y + k) % 4))

    partner = (s, dp_of(other, x, y))
    up_dev = (s + 1, d)
    down_dev = (s - 1, d)

    def remote(src, dst, ssem, rsem, dev):
        return pltpu.make_async_remote_copy(
            src_ref=src, dst_ref=dst, send_sem=ssem, recv_sem=rsem, device_id=dev, device_id_type=MESH
        )

    wcopy = [
        pltpu.make_async_copy(ref, W.at[m, zh, x, y], isem.at[m]) for m, ref in enumerate((wd_in, wu_in))
    ]
    for c in wcopy:
        c.start()

    def col(c):
        return pl.ds(pl.multiple_of(c * ROW, 128), ROW)

    def load_start(src, dst_of, sem):
        @pl.loop(0, ROWS)
        def _(c):
            pltpu.make_async_copy(src.at[:, col(c)], dst_of(c), sem).start()

    load_start(stashed, lambda c: X.at[0, c], isem.at[2])
    load_start(inflow, lambda c: X.at[1, c], isem.at[3])
    load_start(arrive, lambda c: GG.at[c, pl.ds(0, T)], isem.at[4])

    barrier = pltpu.get_barrier_semaphore()
    peers = [along(ax, k) for ax in (0, 1) for k in (1, 2, 3)] + [partner]
    peers += [((s + 1) % 8, d), ((s + 7) % 8, d)]
    for dev in peers:
        pl.semaphore_signal(barrier, inc=1, device_id=dev, device_id_type=MESH)
    pl.semaphore_wait(barrier, len(peers))

    @pl.when(s == 0)
    def _():
        @pl.loop(0, ROWS)
        def _(c):
            pltpu.make_async_copy(entering.at[:, col(c)], A1.at[c], arecv.at[c]).start()

    @pl.when(s == 7)
    def _():
        @pl.loop(0, ROWS)
        def _(c):
            pltpu.make_async_copy(enter.at[:, col(c)], GG.at[c, pl.ds(T, T)], brecv.at[c]).start()

    for c in wcopy:
        c.wait()

    def wreg(m, zz, h, i1, i2, r0=0, nr=HALF):
        rows = pl.ds(HALF * h + r0, nr)
        return W.at[m, zz, i2, i1, rows] if h == 0 else W.at[m, zz, i1, i2, rows]

    ALL = pl.ds(0, 4)
    LO2, HI2 = pl.ds(0, 2), pl.ds(2, 2)

    def axes(h):
        return (1, y, 0, x) if h == 0 else (0, x, 1, y)

    def gmsg(m, w, h, i, into=False):
        zz = zh if w == 0 else other
        a1, o1, a2, o2 = axes(h)
        p1, n1 = (o1 + 1) % 4, (o1 + 3) % 4
        p2, n2 = (o2 + 1) % 4, (o2 + 3) % 4
        f1, f2 = (o1 + 2) % 4, (o2 + 2) % 4
        g = functools.partial(wreg, m, zz, h)
        src, land, axis, k = [
            (lambda: g(o1, o2), lambda: g(n1, o2), a1, 1),
            (lambda: g(o1, o2), lambda: g(p1, o2), a1, 3),
            (lambda: g(n1, o2, 0, NEAR), lambda: g(f1, o2, 0, NEAR), a1, 1),
            (lambda: g(p1, o2, NEAR, FAR), lambda: g(f1, o2, NEAR, FAR), a1, 3),
            (lambda: g(ALL, o2), lambda: g(ALL, n2), a2, 1),
            (lambda: g(ALL, o2), lambda: g(ALL, p2), a2, 3),
            (lambda: g(LO2, n2), lambda: g(LO2, f2), a2, 1),
            (lambda: g(HI2, p2), lambda: g(HI2, f2), a2, 3),
        ][i]
        idx = ((m * 2 + w) * 2 + h) * 8 + i
        ref = land() if into else src()
        return remote(ref, ref, gsend.at[idx], grecv.at[idx], along(axis, k))

    def g_send(m, w, i):
        for h in (0, 1):
            gmsg(m, w, h, i).start()

    def g_step(m, w, got, then):
        for h in (0, 1):
            gmsg(m, w, h, got, True).wait_recv()
            if then is not None:
                gmsg(m, w, h, then).start()

    def g1_start(m, w):
        g_send(m, w, 0)
        g_send(m, w, 1)

    def g1_forward(m, w):
        g_step(m, w, 0, 2)
        g_step(m, w, 1, 3)

    def g2_start(m, w):
        g_step(m, w, 2, None)
        g_step(m, w, 3, None)
        g_send(m, w, 4)
        g_send(m, w, 5)

    def g2_forward(m, w):
        g_step(m, w, 4, 6)
        g_step(m, w, 5, 7)

    def g_done(m, w):
        g_step(m, w, 6, None)
        g_step(m, w, 7, None)

    def zcopy(m):
        own = W.at[m, zh, x, y]
        return remote(own, own, zsend.at[m], zrecv.at[m], partner)

    def zwait(m):
        far = W.at[m, other, x, y]
        remote(far, far, zsend.at[m], zrecv.at[m], partner).wait_recv()

    def gain(c):
        return gin[:, col(c)]

    def norms(src_of, scale_of, dst_of):
        def sq(c, acc):
            v = src_of(c)[...].astype(F32)
            return acc + jnp.sum(v * v, axis=-1, keepdims=True)

        total = lax.fori_loop(0, ROWS, sq, jnp.zeros((T, 1), F32))
        scale_of()[...] = lax.rsqrt(total * (1.0 / D) + EPS)

        @pl.loop(0, ROWS)
        def _(c):
            dst_of(c)[...] = (src_of(c)[...].astype(F32) * scale_of()[...] * gain(c)).astype(BF16)

    def wrow(m, zz, xx):
        return W[m, zz, xx].reshape(ROW, R)

    def latent_half(zz, rows_of, acc):
        @pl.loop(0, 4)
        def _(xx):
            acc[...] += nn(rows_of(zz * 4 + xx), wrow(0, zz, xx))

    def grad_lat_half(zz, k):
        @pl.loop(0, 4)
        def _(xx):
            GL[k] += nn(GG[zz * 4 + xx, pl.ds(k * T, T)], wrow(1, zz, xx))

    def raw_grad(k):
        rows = pl.ds(k * T, T)
        gl, ln, ls = GL[k], LN[rows], LS[rows]
        gn = gl * glat[...]
        m = jnp.mean(gn * ln, axis=-1, keepdims=True)
        raw = (ls * (gn - ln * m)).astype(BF16)
        RAW[rows] = raw
        MT[k] = jnp.sum(raw.astype(F32) * LAT[rows], axis=-1, keepdims=True) * (1.0 / D)
        return jnp.sum(gl * ln, axis=0, keepdims=True)

    def back_row(k, zz, xx):
        c = zz * 4 + xx
        grad_in = nt(RAW[pl.ds(k * T, T)], wrow(0, zz, xx)) * gain(c)
        sc = SC[k]
        in_norm = X[k, c].astype(F32) * sc
        g = GG[c, pl.ds(k * T, T)].astype(F32)
        return (g + sc * (grad_in - in_norm * MT[k])).astype(BF16)

    def act_copy(c):
        return remote(R0.at[c], A1.at[c], asend.at[c], arecv.at[c], up_dev)

    def back_copy(c):
        return remote(B0.at[c], GG.at[c, pl.ds(T, T)], bsend.at[c], brecv.at[c], down_dev)

    def result_half(zz):
        @pl.loop(0, 4)
        def _(xx):
            c = zz * 4 + xx
            R0[c] = (X[1, c].astype(F32) + nt(LO[pl.ds(T, T)], wrow(1, zz, xx))).astype(BF16)

            @pl.when(not_last)
            def _():
                act_copy(c).start()

    for m in (0, 1):
        zcopy(m).start()
        g1_start(m, 0)
    LAT[...] = jnp.zeros_like(LAT)
    GL[...] = jnp.zeros_like(GL)
    pltpu.make_async_copy(X.at[0], X.at[0], isem.at[2]).wait()
    norms(lambda c: X.at[0, c], lambda: SC.at[0], lambda c: N.at[c, pl.ds(0, T)])
    g1_forward(0, 0)
    g1_forward(1, 0)
    g2_start(0, 0)
    pltpu.make_async_copy(X.at[1], X.at[1], isem.at[3]).wait()
    norms(lambda c: X.at[1, c], lambda: SC.at[1], lambda c: N.at[c, pl.ds(T, T)])
    g2_start(1, 0)
    for m in (0, 1):
        zwait(m)
        g1_start(m, 1)
    g2_forward(0, 0)
    g1_forward(0, 1)
    g1_forward(1, 1)
    g2_forward(1, 0)
    g2_start(0, 1)
    g_done(0, 0)
    latent_half(zh, lambda c: N[c], LAT)
    g2_start(1, 1)
    g2_forward(0, 1)
    g_done(1, 0)
    first_half = GG.at[:, pl.ds(0, T)]
    pltpu.make_async_copy(first_half, first_half, isem.at[4]).wait()
    grad_lat_half(zh, 0)
    g2_forward(1, 1)
    g_done(0, 1)
    latent_half(other, lambda c: N[c], LAT)
    lat = LAT[...]
    lat_scale = lax.rsqrt(jnp.mean(lat * lat, axis=-1, keepdims=True) + EPS)
    LS[...] = lat_scale
    LN[...] = lat * lat_scale
    LO[...] = (lat * lat_scale * glat[...]).astype(BF16)
    result_half(zh)
    g_done(1, 1)
    grad_lat_half(other, 0)
    lg0 = raw_grad(0)

    def send_back_half(zz):
        @pl.loop(0, 4)
        def _(xx):
            c = zz * 4 + xx
            B0[c] = back_row(0, zz, xx)

            @pl.when(not_first)
            def _():
                back_copy(c).start()

    send_back_half(other)
    send_back_half(zh)
    result_half(other)

    def greg(m, zz, h, i1, i2, r0=0, nr=HALF):
        rows = pl.ds(HALF * h + r0, nr)
        return G.at[m, zz, i1, i2, rows] if h == 0 else G.at[m, zz, i2, i1, rows]

    def raxes(h):
        return (0, x, 1, y) if h == 0 else (1, y, 0, x)

    def rmsg(m, w, h, i):
        zz = other if w == 0 else zh
        a1, o1, a2, o2 = raxes(h)
        p1, n1, f1 = (o1 + 1) % 4, (o1 + 3) % 4, (o1 + 2) % 4
        p2, n2, f2 = (o2 + 1) % 4, (o2 + 3) % 4, (o2 + 2) % 4
        g = functools.partial(greg, m, zz, h)
        q = (m * 2 + w) * 2 + h
        src, land, axis, k = [
            (lambda: g(f1, LO2), land2.at[q, 0], a1, 1),
            (lambda: g(f1, HI2), land2.at[q, 1], a1, 3),
            (lambda: g(p1, ALL), land4.at[q, 0], a1, 1),
            (lambda: g(n1, ALL), land4.at[q, 1], a1, 3),
            (lambda: g(o1, f2, 0, NEAR), landn.at[q], a2, 1),
            (lambda: g(o1, f2, NEAR, FAR), landf.at[q], a2, 3),
            (lambda: g(o1, p2), land1.at[q, 0], a2, 1),
            (lambda: g(o1, n2), land1.at[q, 1], a2, 3),
        ][i]
        return remote(src(), land, rsend.at[q * 8 + i], rrecv.at[q * 8 + i], along(axis, k))

    def add_into(ref, *lands):
        total = ref[...].astype(F32)
        for land in lands:
            total = total + land[...].astype(F32)
        ref[...] = total.astype(BF16)

    def r_ctx(m, w, h):
        zz = other if w == 0 else zh
        _, o1, _, o2 = raxes(h)
        return functools.partial(greg, m, zz, h), o1, o2, (m * 2 + w) * 2 + h

    def r1_start(m, w):
        for h in (0, 1):
            rmsg(m, w, h, 0).start()
            rmsg(m, w, h, 1).start()

    def r1_relay(m, w):
        for h in (0, 1):
            g, o1, o2, q = r_ctx(m, w, h)
            rmsg(m, w, h, 0).wait_recv()
            add_into(g((o1 + 1) % 4, LO2), land2.at[q, 0])
            rmsg(m, w, h, 2).start()
        for h in (0, 1):
            g, o1, o2, q = r_ctx(m, w, h)
            rmsg(m, w, h, 1).wait_recv()
            add_into(g((o1 + 3) % 4, HI2), land2.at[q, 1])
            rmsg(m, w, h, 3).start()

    def r2_start(m, w):
        for h in (0, 1):
            g, o1, o2, q = r_ctx(m, w, h)
            rmsg(m, w, h, 2).wait_recv()
            rmsg(m, w, h, 3).wait_recv()
            add_into(g(o1, ALL), land4.at[q, 0], land4.at[q, 1])
            rmsg(m, w, h, 4).start()
            rmsg(m, w, h, 5).start()

    def r2_relay(m, w):
        for h in (0, 1):
            g, o1, o2, q = r_ctx(m, w, h)
            rmsg(m, w, h, 4).wait_recv()
            add_into(g(o1, (o2 + 1) % 4, 0, NEAR), landn.at[q])
            rmsg(m, w, h, 6).start()
            rmsg(m, w, h, 5).wait_recv()
            add_into(g(o1, (o2 + 3) % 4, NEAR, FAR), landf.at[q])
            rmsg(m, w, h, 7).start()

    def zgrad(m):
        return remote(G.at[m, other, x, y], landz.at[m], zsend.at[2 + m], zrecv.at[2 + m], partner)

    def r_done(m, w):
        for h in (0, 1):
            g, o1, o2, q = r_ctx(m, w, h)
            rmsg(m, w, h, 6).wait_recv()
            rmsg(m, w, h, 7).wait_recv()
            if w == 0:
                add_into(g(o1, o2), land1.at[q, 0], land1.at[q, 1])
        if w == 0:
            zgrad(m).start()
        else:
            zgrad(m).wait_recv()
            out = out_down if m == 0 else out_up
            for h in (0, 1):
                g, o1, o2, q = r_ctx(m, w, h)
                rows = pl.ds(HALF * h, HALF)
                out[rows] = (
                    g(o1, o2)[...].astype(F32)
                    + land1[q, 0].astype(F32)
                    + land1[q, 1].astype(F32)
                    + landz[m, rows].astype(F32)
                )

    def up_half(zz):
        @pl.loop(0, 4)
        def _(xx):
            c = zz * 4 + xx
            back_copy(c).wait_recv()
            G[1, zz, xx] = tn(GG[c], LO[...]).astype(BF16).reshape(4, UNIT, R)
            GL[1] += nn(GG[c, pl.ds(T, T)], wrow(1, zz, xx))

    def down_half(zz):
        @pl.loop(0, 4)
        def _(xx):
            G[0, zz, xx] = tn(N[zz * 4 + xx], RAW[...]).astype(BF16).reshape(4, UNIT, R)

    def out_copy(src, dst, c, sem):
        return pltpu.make_async_copy(src.at[c], dst.at[:, col(c)], sem)

    def out_back_half(zz):
        @pl.loop(0, 4)
        def _(xx):
            c = zz * 4 + xx
            OB[c] = back_row(1, zz, xx)
            out_copy(OB, out_grad, c, osem.at[1]).start()

    def lmsg(i):
        axis, k = ((1, 1), (1, 2), (1, 3), (0, 1), (0, 2), (0, 3), (None, 0))[i]
        dev = partner if axis is None else along(axis, k)
        stage = 0 if i < 3 else 1 if i < 6 else 2
        return remote(LGP.at[stage], LGL.at[i], lsend.at[i], lrecv.at[i], dev)

    def lg_stage(stage):
        ids = ((0, 1, 2), (3, 4, 5), (6,))[stage]
        total = LGP[stage]
        for i in ids:
            lmsg(i).wait_recv()
            total = total + LGL[i]
        if stage == 2:
            out_lg[...] = total
        else:
            LGP[stage + 1] = total
            for i in ((3, 4, 5), (6,))[stage]:
                lmsg(i).start()

    up_half(other)
    r1_start(1, 0)
    up_half(zh)
    r1_start(1, 1)
    r1_relay(1, 0)
    lg = lg0 + raw_grad(1)
    LGP[0] = jnp.broadcast_to(lg, (8, R))
    for i in (0, 1, 2):
        lmsg(i).start()
    down_half(other)
    r1_start(0, 0)
    r1_relay(1, 1)
    r2_start(1, 0)
    down_half(zh)
    r1_start(0, 1)
    r1_relay(0, 0)
    r2_relay(1, 0)
    r2_start(1, 1)
    r1_relay(0, 1)
    r_done(1, 0)
    r2_relay(1, 1)
    r2_start(0, 0)
    lg_stage(0)
    out_back_half(other)
    r2_relay(0, 0)
    lg_stage(1)
    out_back_half(zh)
    r2_start(0, 1)
    r_done(0, 0)
    r_done(1, 1)
    lg_stage(2)

    @pl.loop(0, ROWS)
    def _(c):
        act_copy(c).wait_recv()

    norms(lambda c: A1.at[c], lambda: SC.at[0], lambda c: N1.at[c])
    r2_relay(0, 1)
    GL[0] = jnp.zeros((T, R), F32)
    latent_half(zh, lambda c: N1[c], GL.at[0])
    latent_half(other, lambda c: N1[c], GL.at[0])
    lat1 = GL[0]
    LO[pl.ds(0, T)] = (
        lat1 * lax.rsqrt(jnp.mean(lat1 * lat1, axis=-1, keepdims=True) + EPS) * glat[...]
    ).astype(BF16)

    @pl.loop(0, ROWS)
    def _(c):
        OA[c] = (A1[c].astype(F32) + nt(LO[pl.ds(0, T)], wrow(1, c // 4, c % 4))).astype(BF16)
        out_copy(OA, out_act, c, osem.at[0]).start()

    r_done(0, 1)

    for m in (0, 1):
        zcopy(m).wait_send()
        zgrad(m).wait_send()
        for w in (0, 1):
            for h in (0, 1):
                for i in range(8):
                    gmsg(m, w, h, i).wait_send()
                    rmsg(m, w, h, i).wait_send()
    for i in range(7):
        lmsg(i).wait_send()

    @pl.when(not_last)
    def _():
        @pl.loop(0, ROWS)
        def _(c):
            act_copy(c).wait_send()

    @pl.when(not_first)
    def _():
        @pl.loop(0, ROWS)
        def _(c):
            back_copy(c).wait_send()

    pltpu.make_async_copy(OA, OA, osem.at[0]).wait()
    pltpu.make_async_copy(OB, OB, osem.at[1]).wait()


def on_device(
    inflow, entering, arrive_grad, enter_grad, stashed, w_down, w_up, norm_gain, latent_gain
):
    d = lax.axis_index("dp")
    anyspace = pl.BlockSpec(memory_space=pl.ANY)
    vmem = pl.BlockSpec(memory_space=pltpu.VMEM)
    rows = (ROWS, T, ROW)
    dma = pltpu.SemaphoreType.DMA
    acts, grads, down, up, lg = pl.pallas_call(
        kernel,
        out_shape=(
            jax.ShapeDtypeStruct((T, D), BF16),
            jax.ShapeDtypeStruct((T, D), BF16),
            jax.ShapeDtypeStruct((UNIT, R), F32),
            jax.ShapeDtypeStruct((UNIT, R), F32),
            jax.ShapeDtypeStruct((8, R), F32),
        ),
        in_specs=[anyspace] * 7 + [vmem] * 2,
        out_specs=(anyspace, anyspace, vmem, vmem, vmem),
        scratch_shapes=[
            pltpu.VMEM((2, 2, 4, 4, UNIT, R), BF16),
            pltpu.VMEM((2, 2, 4, 4, UNIT, R), BF16),
            pltpu.VMEM((2,) + rows, BF16),
            pltpu.VMEM((ROWS, 2 * T, ROW), BF16),
            pltpu.VMEM((ROWS, 2 * T, ROW), BF16),
            pltpu.VMEM(rows, BF16),
            pltpu.VMEM(rows, BF16),
            pltpu.VMEM(rows, BF16),
            pltpu.VMEM(rows, BF16),
            pltpu.VMEM(rows, BF16),
            pltpu.VMEM(rows, BF16),
            pltpu.VMEM((8, 2, 4, HALF, R), BF16),
            pltpu.VMEM((8, 2, 2, HALF, R), BF16),
            pltpu.VMEM((8, NEAR, R), BF16),
            pltpu.VMEM((8, FAR, R), BF16),
            pltpu.VMEM((8, 2, HALF, R), BF16),
            pltpu.VMEM((2, UNIT, R), BF16),
            pltpu.VMEM((2 * T, R), F32),
            pltpu.VMEM((2 * T, R), F32),
            pltpu.VMEM((2 * T, 1), F32),
            pltpu.VMEM((2 * T, R), BF16),
            pltpu.VMEM((2, T, R), F32),
            pltpu.VMEM((2 * T, R), BF16),
            pltpu.VMEM((2, T, 1), F32),
            pltpu.VMEM((2, T, 1), F32),
            pltpu.VMEM((3, 8, R), F32),
            pltpu.VMEM((7, 8, R), F32),
            dma((64,)), dma((64,)),
            dma((4,)), dma((4,)),
            dma((64,)), dma((64,)),
            dma((ROWS,)), dma((ROWS,)),
            dma((ROWS,)), dma((ROWS,)),
            dma((7,)), dma((7,)),
            dma((5,)), dma((2,)),
        ],
        compiler_params=pltpu.CompilerParams(
            collective_id=0, has_side_effects=True, vmem_limit_bytes=60 * 1024 * 1024
        ),
        name="relay",
    )(
        inflow[0], entering[0], arrive_grad[0], enter_grad[0], stashed[0],
        w_down[0], w_up[0].T, norm_gain, latent_gain,
    )
    own_gain = lax.dynamic_slice(norm_gain, (0, d * UNIT), (1, UNIT))
    gin = jnp.sum(w_down[0].astype(F32) * down, axis=-1)[None] / own_gain
    glat = lax.dynamic_slice(lg, (0, d * 8), (1, 8))
    return acts[None], grads[None], down[None], up.T[None], gin, glat


def solution(mesh):
    in_specs = (
        P("section", "dp", None),
        P(None, "dp", None),
        P("section", "dp", None),
        P(None, "dp", None),
        P("section", "dp", None),
        P("section", "dp", None),
        P("section", None, "dp"),
        P("section", None),
        P("section", None),
    )
    out_specs = (
        P("section", "dp", None),
        P("section", "dp", None),
        P("section", "dp", None),
        P("section", None, "dp"),
        P("section", "dp"),
        P("section", "dp"),
    )
    return jax.shard_map(
        on_device, mesh=mesh, in_specs=in_specs, out_specs=out_specs, check_vma=False
    )
```

time: 832 us -> 126 us (0.15); the launches traced: 816 us -> 125 us
  waiting for transfers between devices: 499 us -> 0 us
  blocking collectives: 240 us -> 0 us
  Pallas kernels: 0 us -> 115 us
  matrix products: 37.9 us -> 0 us
  between operations: 15.3 us -> 0.67 us
  other arithmetic: 11.9 us -> 2.38 us
    reduce_scatter x2 -> x0, waiting for transfers between devices: 270 us -> none  [the longest x1 270 us: on_device(): lax.psum_scatter(totals[1], 'dp', scatter_dimension=1, tiled=True)]
    unnamed x1 -> x0, blocking collectives: 240 us -> none
    all_gather x2 -> x0, waiting for transfers between devices: 211 us -> none  [the longest x1 110 us: on_device(): lax.all_gather(w_down, 'dp', axis=1, tiled=True)]
    pallas_call x0 -> x1, Pallas kernels: none -> 115 us  [on_device(): pl.pallas_call(kernel, out_shape=(jax.ShapeDtypeStruct((T, D), BF16), jax...]
    dot_general x13 -> x0, matrix products: 37.9 us -> none  [the longest x2 7.13 us: forward_block(): jnp.dot(lat_out, upward, preferred_element_type=jnp.float32)]
    ppermute x2 -> x0, waiting for transfers between devices: 16.6 us -> none  [passed_along(): lax.ppermute(value, axis, [(source, source + steps) for source in range(f...]
  transfers between devices with their start and end apart: 6 -> 0, of which waited for: 4 -> 0; matrix products, arithmetic and copies ran while one was open for 5% -> 0% of each run, Pallas kernels for 0% -> 0%
where the time goes in v1:
time: 126 us; the launch traced here: 125 us
  Pallas kernels  115 us (91%)
  local copies, waits for them, and re-layouts  6.86 us (5%)
  other arithmetic  2.38 us (2%)
    pallas_call x1, Pallas kernels, on_device(): pl.pallas_call(kernel, out_shape=(jax.ShapeDtypeStruct((T, D), BF16), jax...  115 us
    unnamed x12, local copies, waits for them, and re-layouts  5.6 us

profile of v1, /device:TPU:1, one launch (start us, length us, event | category | flops | bytes accessed | tf_op | source)
XLA Modules:
  0.0 125.3 jit_solution(3951874667001279078)
XLA Ops:
  0.6 0.0 copy-start.2
  0.6 115.4 %relay.1 = (bf16[128,7168]{1,0:T(8,128)(2,1)}, bf16[128,7168]{1,0:T(8,128)(2,1)}, f32[224,256]{1,0:T(8,128)}, f32[224,256]{1,0:T(8,128)}, f32[8,256]{1,0:T(8,128)}) custom-call(bf16[128,7168]{1,0:T(8,128)(2,1)} %bitcast.19, bf16[128,7168]{1,0:T(8,128)(2,1)} %bitcast.20, bf16[128,7168]{1,0:T(8,128)(2,1)} %bitcast.21, bf16[128,7168]{1,0:T(8,128)(2,1)} %bitcast.22, ...), custom_call_target="tpu_custom_call" | custom-call | tf_op jit(solution)/shard_map/relay/pallas_call | solution.py:530
  116.1 1.3 %constant_dynamic-slice_fusion = f32[1,8]{1,0:T(1,128)} fusion(f32[8,256]{1,0:T(8,128)} %get-tuple-element.15, s32[]{:T(128)S(6)} %select_n.7), kind=kLoop, calls=%fused_computation.2 | loop fusion | bytes 68 | tf_op jit(solution)/shard_map/dynamic_slice | solution.py:587
  117.3 0.0 copy-done.2
  117.3 1.1 multiply_reduce_fusion
  118.4 1.3 %dynamic-slice_divide_fusion = f32[1,224]{1,0:T(1,128)} fusion(f32[1,224]{1,0:T(1,128)S(1)} %bitcast.28, f32[1,7168]{1,0:T(1,128)} %gin.1, s32[]{:T(128)S(6)} %select_n.6), kind=kLoop, calls=%fused_computation.1 | loop fusion | flops 224 | bytes 2692 | tf_op jit(solution)/shard_map/div | solution.py:586
  119.7 0.0 copy-start
  119.7 3.0 %copy.19 = bf16[1,128,7168]{2,1,0:T(8,128)(2,1)} copy(bf16[1,128,7168]{2,1,0:T(8,128)(2,1)} %bitcast.18) | data formatting | bytes 3670016
  122.7 0.0 copy-done
  122.7 0.0 copy-start.1
  122.7 0.0 copy-start.3
  122.7 1.2 copy.20
  124.0 0.0 copy-done.1
  124.0 0.7 copy.21
  124.6 0.0 copy-done.3
  124.6 0.7 copy.22
Async XLA Ops:
  0.6 116.7 %copy-start.2 = (bf16[1,224,256]{2,1,0:T(8,128)(2,1)S(1)}, bf16[1,224,256]{2,1,0:T(8,128)(2,1)}, u32[]{:S(2)}) copy-start(bf16[1,224,256]{2,1,0:T(8,128)(2,1)} %param.14) | copy-start | bytes 344068
  119.7 3.0 %copy-start = (bf16[128,7168]{1,0:T(8,128)(2,1)S(1)}, bf16[128,7168]{1,0:T(8,128)(2,1)}, u32[]{:S(2)}) copy-start(bf16[128,7168]{1,0:T(8,128)(2,1)} %get-tuple-element.12) | copy-start | bytes 5505028
  122.7 1.2 copy-start.1
  122.7 1.9 %copy-start.3 = (f32[224,256]{1,0:T(8,128)S(1)}, f32[224,256]{1,0:T(8,128)}, u32[]{:S(2)}) copy-start(f32[224,256]{1,0:T(8,128)} %get-tuple-element.14) | copy-start | bytes 688132

commit v2 on v1

--- a/solution.py
+++ b/solution.py
@@ -42,7 +42,7 @@
     land4, land2, landn, landf, land1, landz,
     LAT, LN, LS, LO, GL, RAW, MT, SC, LGP, LGL,
     gsend, grecv, zsend, zrecv, rsend, rrecv, asend, arecv, bsend, brecv,
-    lsend, lrecv, isem, osem,
+    lsend, lrecv, isem, osem, go,
 ):
     s = lax.axis_index("section")
     d = lax.axis_index("dp")
@@ -50,6 +50,7 @@
     x = (d // 4) % 4
     y = d % 4
     other = 1 - zh
+    core = s % 2
     not_last = s < 7
     not_first = s > 0
 
@@ -217,7 +218,7 @@
         raw = (ls * (gn - ln * m)).astype(BF16)
         RAW[rows] = raw
         MT[k] = jnp.sum(raw.astype(F32) * LAT[rows], axis=-1, keepdims=True) * (1.0 / D)
-        return jnp.sum(gl * ln, axis=0, keepdims=True)
+        LGP[0] += jnp.broadcast_to(jnp.sum(gl * ln, axis=0, keepdims=True), (8, R))
 
     def back_row(k, zz, xx):
         c = zz * 4 + xx
@@ -243,48 +244,6 @@
             def _():
                 act_copy(c).start()
 
-    for m in (0, 1):
-        zcopy(m).start()
-        g1_start(m, 0)
-    LAT[...] = jnp.zeros_like(LAT)
-    GL[...] = jnp.zeros_like(GL)
-    pltpu.make_async_copy(X.at[0], X.at[0], isem.at[2]).wait()
-    norms(lambda c: X.at[0, c], lambda: SC.at[0], lambda c: N.at[c, pl.ds(0, T)])
-    g1_forward(0, 0)
-    g1_forward(1, 0)
-    g2_start(0, 0)
-    pltpu.make_async_copy(X.at[1], X.at[1], isem.at[3]).wait()
-    norms(lambda c: X.at[1, c], lambda: SC.at[1], lambda c: N.at[c, pl.ds(T, T)])
-    g2_start(1, 0)
-    for m in (0, 1):
-        zwait(m)
-        g1_start(m, 1)
-    g2_forward(0, 0)
-    g1_forward(0, 1)
-    g1_forward(1, 1)
-    g2_forward(1, 0)
-    g2_start(0, 1)
-    g_done(0, 0)
-    latent_half(zh, lambda c: N[c], LAT)
-    g2_start(1, 1)
-    g2_forward(0, 1)
-    g_done(1, 0)
-    first_half = GG.at[:, pl.ds(0, T)]
-    pltpu.make_async_copy(first_half, first_half, isem.at[4]).wait()
-    grad_lat_half(zh, 0)
-    g2_forward(1, 1)
-    g_done(0, 1)
-    latent_half(other, lambda c: N[c], LAT)
-    lat = LAT[...]
-    lat_scale = lax.rsqrt(jnp.mean(lat * lat, axis=-1, keepdims=True) + EPS)
-    LS[...] = lat_scale
-    LN[...] = lat * lat_scale
-    LO[...] = (lat * lat_scale * glat[...]).astype(BF16)
-    result_half(zh)
-    g_done(1, 1)
-    grad_lat_half(other, 0)
-    lg0 = raw_grad(0)
-
     def send_back_half(zz):
         @pl.loop(0, 4)
         def _(xx):
@@ -294,10 +253,6 @@
             @pl.when(not_first)
             def _():
                 back_copy(c).start()
-
-    send_back_half(other)
-    send_back_half(zh)
-    result_half(other)
 
     def greg(m, zz, h, i1, i2, r0=0, nr=HALF):
         rows = pl.ds(HALF * h + r0, nr)
@@ -403,7 +358,6 @@
             c = zz * 4 + xx
             back_copy(c).wait_recv()
             G[1, zz, xx] = tn(GG[c], LO[...]).astype(BF16).reshape(4, UNIT, R)
-            GL[1] += nn(GG[c, pl.ds(T, T)], wrow(1, zz, xx))
 
     def down_half(zz):
         @pl.loop(0, 4)
@@ -425,6 +379,10 @@
         dev = partner if axis is None else along(axis, k)
         stage = 0 if i < 3 else 1 if i < 6 else 2
         return remote(LGP.at[stage], LGL.at[i], lsend.at[i], lrecv.at[i], dev)
+
+    def lg_start():
+        for i in (0, 1, 2):
+            lmsg(i).start()
 
     def lg_stage(stage):
         ids = ((0, 1, 2), (3, 4, 5), (6,))[stage]
@@ -439,58 +397,175 @@
             for i in ((3, 4, 5), (6,))[stage]:
                 lmsg(i).start()
 
-    up_half(other)
-    r1_start(1, 0)
-    up_half(zh)
-    r1_start(1, 1)
-    r1_relay(1, 0)
-    lg = lg0 + raw_grad(1)
-    LGP[0] = jnp.broadcast_to(lg, (8, R))
-    for i in (0, 1, 2):
-        lmsg(i).start()
-    down_half(other)
-    r1_start(0, 0)
-    r1_relay(1, 1)
-    r2_start(1, 0)
-    down_half(zh)
-    r1_start(0, 1)
-    r1_relay(0, 0)
-    r2_relay(1, 0)
-    r2_start(1, 1)
-    r1_relay(0, 1)
-    r_done(1, 0)
-    r2_relay(1, 1)
-    r2_start(0, 0)
-    lg_stage(0)
-    out_back_half(other)
-    r2_relay(0, 0)
-    lg_stage(1)
-    out_back_half(zh)
-    r2_start(0, 1)
-    r_done(0, 0)
-    r_done(1, 1)
-    lg_stage(2)
-
-    @pl.loop(0, ROWS)
-    def _(c):
-        act_copy(c).wait_recv()
-
-    norms(lambda c: A1.at[c], lambda: SC.at[0], lambda c: N1.at[c])
-    r2_relay(0, 1)
-    GL[0] = jnp.zeros((T, R), F32)
-    latent_half(zh, lambda c: N1[c], GL.at[0])
-    latent_half(other, lambda c: N1[c], GL.at[0])
-    lat1 = GL[0]
-    LO[pl.ds(0, T)] = (
-        lat1 * lax.rsqrt(jnp.mean(lat1 * lat1, axis=-1, keepdims=True) + EPS) * glat[...]
-    ).astype(BF16)
-
-    @pl.loop(0, ROWS)
-    def _(c):
-        OA[c] = (A1[c].astype(F32) + nt(LO[pl.ds(0, T)], wrow(1, c // 4, c % 4))).astype(BF16)
-        out_copy(OA, out_act, c, osem.at[0]).start()
-
-    r_done(0, 1)
+    def forward_next():
+        @pl.loop(0, ROWS)
+        def _(c):
+            act_copy(c).wait_recv()
+
+        norms(lambda c: A1.at[c], lambda: SC.at[0], lambda c: N1.at[c])
+        GL[0] = jnp.zeros((T, R), F32)
+        latent_half(zh, lambda c: N1[c], GL.at[0])
+        latent_half(other, lambda c: N1[c], GL.at[0])
+        lat1 = GL[0]
+        LO[pl.ds(0, T)] = (
+            lat1 * lax.rsqrt(jnp.mean(lat1 * lat1, axis=-1, keepdims=True) + EPS) * glat[...]
+        ).astype(BF16)
+
+        @pl.loop(0, ROWS)
+        def _(c):
+            OA[c] = (A1[c].astype(F32) + nt(LO[pl.ds(0, T)], wrow(1, c // 4, c % 4))).astype(BF16)
+            out_copy(OA, out_act, c, osem.at[0]).start()
+
+    LAT[...] = jnp.zeros_like(LAT)
+    GL[...] = jnp.zeros_like(GL)
+    LGP[0] = jnp.zeros((8, R), F32)
+    for m in (0, 1):
+        zcopy(m).start()
+
+    @pl.when(core == 0)
+    def _():
+        g1_start(0, 0)
+        g1_start(1, 0)
+
+    pltpu.make_async_copy(X.at[0], X.at[0], isem.at[2]).wait()
+    norms(lambda c: X.at[0, c], lambda: SC.at[0], lambda c: N.at[c, pl.ds(0, T)])
+
+    @pl.when(core == 0)
+    def _():
+        g1_forward(0, 0)
+        g1_forward(1, 0)
+        g2_start(0, 0)
+        g2_start(1, 0)
+
+    pltpu.make_async_copy(X.at[1], X.at[1], isem.at[3]).wait()
+    norms(lambda c: X.at[1, c], lambda: SC.at[1], lambda c: N.at[c, pl.ds(T, T)])
+    first_half = GG.at[:, pl.ds(0, T)]
+    pltpu.make_async_copy(first_half, first_half, isem.at[4]).wait()
+
+    @pl.when(core == 1)
+    def _():
+        pl.semaphore_wait(go, 1)
+        g1_start(0, 0)
+        g1_start(1, 0)
+        g1_forward(0, 0)
+        g1_forward(1, 0)
+        g2_start(0, 0)
+        g2_start(1, 0)
+
+    for m in (0, 1):
+        zwait(m)
+        g1_start(m, 1)
+    g2_forward(0, 0)
+    g1_forward(0, 1)
+    g1_forward(1, 1)
+    g2_forward(1, 0)
+    g2_start(0, 1)
+    g2_start(1, 1)
+
+    @pl.when(core == 0)
+    def _():
+        pl.semaphore_signal(go, inc=1, device_id=up_dev, device_id_type=MESH)
+
+    g_done(0, 0)
+    latent_half(zh, lambda c: N[c], LAT)
+    g2_forward(0, 1)
+    g_done(1, 0)
+    grad_lat_half(zh, 0)
+    g2_forward(1, 1)
+    g_done(0, 1)
+    latent_half(other, lambda c: N[c], LAT)
+    lat = LAT[...]
+    lat_scale = lax.rsqrt(jnp.mean(lat * lat, axis=-1, keepdims=True) + EPS)
+    LS[...] = lat_scale
+    LN[...] = lat * lat_scale
+    LO[...] = (lat * lat_scale * glat[...]).astype(BF16)
+    result_half(zh)
+
+    @pl.when(core == 0)
+    def _():
+        g_done(1, 1)
+        grad_lat_half(other, 0)
+        raw_grad(0)
+        send_back_half(other)
+        send_back_half(zh)
+        result_half(other)
+        up_half(other)
+        r1_start(1, 0)
+        up_half(zh)
+        r1_start(1, 1)
+        r1_relay(1, 0)
+        grad_lat_half(other, 1)
+        grad_lat_half(zh, 1)
+        raw_grad(1)
+        lg_start()
+        down_half(other)
+        r1_start(0, 0)
+        r1_relay(1, 1)
+        r2_start(1, 0)
+        down_half(zh)
+        r1_start(0, 1)
+        r1_relay(0, 0)
+        r2_relay(1, 0)
+        r2_start(1, 1)
+        r1_relay(0, 1)
+        r_done(1, 0)
+        r2_relay(1, 1)
+        r2_start(0, 0)
+        lg_stage(0)
+        out_back_half(other)
+        r2_relay(0, 0)
+        lg_stage(1)
+        out_back_half(zh)
+        r2_start(0, 1)
+        r_done(0, 0)
+        r_done(1, 1)
+        lg_stage(2)
+        r2_relay(0, 1)
+        forward_next()
+        r_done(0, 1)
+
+    @pl.when(core == 1)
+    def _():
+        up_half(other)
+        r1_start(1, 0)
+        g_done(1, 1)
+        grad_lat_half(other, 0)
+        raw_grad(0)
+        r1_relay(1, 0)
+        send_back_half(other)
+        up_half(zh)
+        r1_start(1, 1)
+        r2_start(1, 0)
+        send_back_half(zh)
+        r1_relay(1, 1)
+        grad_lat_half(other, 1)
+        grad_lat_half(zh, 1)
+        raw_grad(1)
+        lg_start()
+        down_half(other)
+        r1_start(0, 0)
+        r2_relay(1, 0)
+        r2_start(1, 1)
+        r1_relay(0, 0)
+        result_half(other)
+        down_half(zh)
+        r1_start(0, 1)
+        r_done(1, 0)
+        r2_relay(1, 1)
+        r2_start(0, 0)
+        r1_relay(0, 1)
+        lg_stage(0)
+        out_back_half(other)
+        r2_relay(0, 0)
+        r_done(1, 1)
+        lg_stage(1)
+        r2_start(0, 1)
+        out_back_half(zh)
+        r_done(0, 0)
+        lg_stage(2)
+        r2_relay(0, 1)
+        forward_next()
+        r_done(0, 1)
 
     for m in (0, 1):
         zcopy(m).wait_send()
@@ -519,10 +594,30 @@
     pltpu.make_async_copy(OB, OB, osem.at[1]).wait()
 
 
+def finish(acts, grads, down, up, lg, wd, gain, o_acts, o_grads, o_down, o_up, o_gin, o_glat, sem, pad):
+    d = lax.axis_index("dp")
+    for i, (src, dst) in enumerate(((acts, o_acts), (grads, o_grads))):
+        for j in range(8):
+            rows = pl.ds(16 * j, 16)
+            pltpu.make_async_copy(src.at[rows], dst.at[rows], sem.at[i]).start()
+    o_down[...] = down[...]
+    o_up[...] = up[...]
+    pad[pl.ds(0, UNIT)] = down[...] * wd[...].astype(F32)
+    pad[pl.ds(UNIT, R - UNIT)] = jnp.zeros((R - UNIT, R), F32)
+    sums = jnp.sum(pad[...].T, axis=0, keepdims=True)
+    first = d * UNIT
+    start = pl.multiple_of(jnp.minimum(first // 128 * 128, D - 384), 128)
+    window = jnp.broadcast_to(gain[:, pl.ds(start, 384)], (8, 384))
+    own = pltpu.roll(window, (384 - (first - start)) % 384, 1)
+    o_gin[...] = sums[:, :UNIT] / own[0:1, :UNIT]
+    o_glat[...] = pltpu.roll(lg[...], (R - 8 * d) % R, 1)[0:1, :8]
+    pltpu.make_async_copy(acts, o_acts, sem.at[0]).wait()
+    pltpu.make_async_copy(grads, o_grads, sem.at[1]).wait()
+
+
 def on_device(
     inflow, entering, arrive_grad, enter_grad, stashed, w_down, w_up, norm_gain, latent_gain
 ):
-    d = lax.axis_index("dp")
     anyspace = pl.BlockSpec(memory_space=pl.ANY)
     vmem = pl.BlockSpec(memory_space=pltpu.VMEM)
     rows = (ROWS, T, ROW)
@@ -573,6 +668,7 @@
             dma((ROWS,)), dma((ROWS,)),
             dma((7,)), dma((7,)),
             dma((5,)), dma((2,)),
+            pltpu.SemaphoreType.REGULAR,
         ],
         compiler_params=pltpu.CompilerParams(
             collective_id=0, has_side_effects=True, vmem_limit_bytes=60 * 1024 * 1024
@@ -582,9 +678,22 @@
         inflow[0], entering[0], arrive_grad[0], enter_grad[0], stashed[0],
         w_down[0], w_up[0].T, norm_gain, latent_gain,
     )
-    own_gain = lax.dynamic_slice(norm_gain, (0, d * UNIT), (1, UNIT))
-    gin = jnp.sum(w_down[0].astype(F32) * down, axis=-1)[None] / own_gain
-    glat = lax.dynamic_slice(lg, (0, d * 8), (1, 8))
+    outs = pl.pallas_call(
+        finish,
+        out_shape=(
+            jax.ShapeDtypeStruct((T, D), BF16),
+            jax.ShapeDtypeStruct((T, D), BF16),
+            jax.ShapeDtypeStruct((UNIT, R), F32),
+            jax.ShapeDtypeStruct((UNIT, R), F32),
+            jax.ShapeDtypeStruct((1, UNIT), F32),
+            jax.ShapeDtypeStruct((1, 8), F32),
+        ),
+        in_specs=[anyspace] * 2 + [vmem] * 5,
+        out_specs=(anyspace,) * 2 + (vmem,) * 4,
+        scratch_shapes=[dma((2,)), pltpu.VMEM((R, R), F32)],
+        name="finish",
+    )(acts, grads, down, up, lg, w_down[0], norm_gain)
+    acts, grads, down, up, gin, glat = outs
     return acts[None], grads[None], down[None], up.T[None], gin, glat
 
 

time: 126 us -> 237 us (1.88)
  the two profiles are of different devices: /device:TPU:1 before, /device:TPU:32 now
where the time goes in v2:
time: 237 us; the launch traced here: 236 us
  Pallas kernels  236 us (100%)
    pallas_call x1, Pallas kernels, on_device(): pl.pallas_call(kernel, out_shape=(jax.ShapeDtypeStruct((T, D), BF16), jax...  121 us
    pallas_call x1, Pallas kernels, on_device(): pl.pallas_call(finish, out_shape=(jax.ShapeDtypeStruct((T, D), BF16), jax...  114 us

profile of v2, /device:TPU:32, one launch (start us, length us, event | category | flops | bytes accessed | tf_op | source)
XLA Modules:
  0.0 236.4 jit_solution(6874260642957914777)
XLA Ops:
  0.6 121.4 %relay.1 = (bf16[128,7168]{1,0:T(8,128)(2,1)}, bf16[128,7168]{1,0:T(8,128)(2,1)}, f32[224,256]{1,0:T(8,128)}, f32[224,256]{1,0:T(8,128)}, f32[8,256]{1,0:T(8,128)}) custom-call(bf16[128,7168]{1,0:T(8,128)(2,1)} %bitcast.15, bf16[128,7168]{1,0:T(8,128)(2,1)} %bitcast.16, bf16[128,7168]{1,0:T(8,128)(2,1)} %bitcast.17, bf16[128,7168]{1,0:T(8,128)(2,1)} %bitcast.18, ...), custom_call_target="tpu_custom_call" | custom-call | tf_op jit(solution)/shard_map/relay/pallas_call | solution.py:625
  122.1 114.2 %finish.1 = (bf16[128,7168]{1,0:T(8,128)(2,1)}, bf16[128,7168]{1,0:T(8,128)(2,1)}, f32[224,256]{1,0:T(8,128)}, f32[224,256]{1,0:T(8,128)}, f32[1,224]{1,0:T(1,128)}, /*index=5*/f32[1,8]{1,0:T(1,128)}) custom-call(bf16[128,7168]{1,0:T(8,128)(2,1)} %get-tuple-element.17.acts, bf16[128,7168]{1,0:T(8,128)(2,1)} %get-tuple-element.18.grads, ...), custom_call_target="tpu_custom_call" | custom-call | tf_op jit(solution)/shard_map/finish/pallas_call | solution.py:681

commit v3 on v2

v3 whole, which is shorter than its diff:
```python
import functools

import jax
import jax.numpy as jnp
from jax import lax
from jax.experimental import pallas as pl
from jax.experimental.pallas import tpu as pltpu
from jax.sharding import PartitionSpec as P

EPS = 1e-06
MESH = pl.DeviceIdType.MESH
F32 = jnp.float32
BF16 = jnp.bfloat16

D = 7168
R = 256
T = 128
UNIT = 224
HALF = 112
NEAR = 64
FAR = HALF - NEAR
ROW = 4 * UNIT
ROWS = D // ROW


def nt(a, b):
    return lax.dot_general(a, b, (((1,), (1,)), ((), ())), preferred_element_type=F32)


def tn(a, b):
    return lax.dot_general(a, b, (((0,), (0,)), ((), ())), preferred_element_type=F32)


def nn(a, b):
    return jnp.dot(a, b, preferred_element_type=F32)


def kernel(
    inflow, entering, arrive, enter, stashed, wd_in, wu_in, gin, glat,
    out_act, out_grad, out_down, out_up, out_lg,
    W, G, X, N, NT, GG, A1, N1, R0, B0, OA, OB,
    land_a, land_b, landn, landf, landu, land1, landz,
    LAT, LN, LS, LO, LO1, GL, RAW, MT, SC, LGP, LGL,
    gsend, grecv, zsend, zrecv, rsend, rrecv, asend, arecv, bsend, brecv,
    lsend, lrecv, isem, osem,
):
    s = lax.axis_index("section")
    d = lax.axis_index("dp")
    zh = d // 16
    x = (d // 4) % 4
    y = d % 4
    other = 1 - zh
    core = s % 2
    not_last = s < 7
    not_first = s > 0

    def dp_of(zz, xx, yy):
        return zz * 16 + xx * 4 + yy

    def along(axis, k):
        if axis == 0:
            return (s, dp_of(zh, (x + k) % 4, y))
        return (s, dp_of(zh, x, (y + k) % 4))

    partner = (s, dp_of(other, x, y))
    up_dev = (s + 1, d)
    down_dev = (s - 1, d)

    def remote(src, dst, ssem, rsem, dev):
        return pltpu.make_async_remote_copy(
            src_ref=src, dst_ref=dst, send_sem=ssem, recv_sem=rsem, device_id=dev, device_id_type=MESH
        )

    wcopy = [
        pltpu.make_async_copy(ref, W.at[m, zh, x, y], isem.at[m]) for m, ref in enumerate((wd_in, wu_in))
    ]
    for c in wcopy:
        c.start()

    def col(c):
        return pl.ds(pl.multiple_of(c * ROW, 128), ROW)

    def load_start(src, dst_of, sem):
        @pl.loop(0, ROWS)
        def _(c):
            pltpu.make_async_copy(src.at[:, col(c)], dst_of(c), sem).start()

    load_start(stashed, lambda c: X.at[0, c], isem.at[2])
    load_start(inflow, lambda c: X.at[1, c], isem.at[3])
    load_start(arrive, lambda c: GG.at[c, pl.ds(0, T)], isem.at[4])

    barrier = pltpu.get_barrier_semaphore()
    peers = [along(ax, k) for ax in (0, 1) for k in (1, 2, 3)] + [partner]
    peers += [((s + 1) % 8, d), ((s + 7) % 8, d)]
    for dev in peers:
        pl.semaphore_signal(barrier, inc=1, device_id=dev, device_id_type=MESH)
    pl.semaphore_wait(barrier, len(peers))

    @pl.when(s == 0)
    def _():
        @pl.loop(0, ROWS)
        def _(c):
            pltpu.make_async_copy(entering.at[:, col(c)], A1.at[c], arecv.at[c]).start()

    @pl.when(s == 7)
    def _():
        @pl.loop(0, ROWS)
        def _(c):
            pltpu.make_async_copy(enter.at[:, col(c)], GG.at[c, pl.ds(T, T)], brecv.at[c]).start()

    for c in wcopy:
        c.wait()

    def wreg(m, zz, h, i1, i2):
        rows = pl.ds(HALF * h, HALF)
        return W.at[m, zz, i2, i1, rows] if h == 0 else W.at[m, zz, i1, i2, rows]

    def gmsg(m, w, h, i, into=False):
        zz = zh if w == 0 else other
        a1, o1, a2, o2 = (1, y, 0, x) if h == 0 else (0, x, 1, y)
        n2, p2, f2 = (o2 + 3) % 4, (o2 + 1) % 4, (o2 + 2) % 4
        k = i + 1 if i < 3 else (i - 3) % 4
        unit = (o1 + (0, 3, 1, 2)[k]) % 4
        if i < 3:
            src, land, axis, step = (o1, o2), (unit, o2), a1, (1, 3, 2)[i]
        elif i < 7:
            src, land, axis, step = (unit, o2), (unit, n2), a2, 1
        elif i < 11:
            src, land, axis, step = (unit, o2), (unit, p2), a2, 3
        elif k in (0, 3):
            src, land, axis, step = (unit, n2), (unit, f2), a2, 1
        else:
            src, land, axis, step = (unit, p2), (unit, f2), a2, 3
        idx = ((m * 2 + w) * 2 + h) * 15 + i
        ref = wreg(m, zz, h, *(land if into else src))
        return remote(ref, ref, gsend.at[idx], grecv.at[idx], along(axis, step))

    def g_start(m, w):
        for i in (0, 1, 2, 3, 7):
            for h in (0, 1):
                gmsg(m, w, h, i).start()

    def g_first(m, w):
        for k in (1, 2, 3):
            for h in (0, 1):
                gmsg(m, w, h, k - 1, True).wait_recv()
                gmsg(m, w, h, 3 + k).start()
                gmsg(m, w, h, 7 + k).start()

    def g_second(m, w, ks=(0, 1, 2, 3)):
        for k in ks:
            for h in (0, 1):
                gmsg(m, w, h, (3 if k in (0, 3) else 7) + k, True).wait_recv()
                gmsg(m, w, h, 11 + k).start()

    def g_done(m, w):
        for k in range(4):
            for h in (0, 1):
                gmsg(m, w, h, (7 if k in (0, 3) else 3) + k, True).wait_recv()
                gmsg(m, w, h, 11 + k, True).wait_recv()

    def zcopy(m):
        own = W.at[m, zh, x, y]
        return remote(own, own, zsend.at[m], zrecv.at[m], partner)

    def zwait(m):
        far = W.at[m, other, x, y]
        remote(far, far, zsend.at[m], zrecv.at[m], partner).wait_recv()

    def gain(c):
        return gin[:, col(c)]

    def norms(src_of, scale_of, dst_of):
        def sq(c, acc):
            v = src_of(c)[...].astype(F32)
            return acc + jnp.sum(v * v, axis=-1, keepdims=True)

        total = lax.fori_loop(0, ROWS, sq, jnp.zeros((T, 1), F32))
        scale_of()[...] = lax.rsqrt(total * (1.0 / D) + EPS)

        @pl.loop(0, ROWS)
        def _(c):
            dst_of(c)[...] = (src_of(c)[...].astype(F32) * scale_of()[...] * gain(c)).astype(BF16)

    def wrow(m, zz, xx):
        return W[m, zz, xx].reshape(ROW, R)

    def latent_half(zz, rows_of, acc):
        @pl.loop(0, 4)
        def _(xx):
            acc[...] += nn(rows_of(zz * 4 + xx), wrow(0, zz, xx))

    def grad_lat_half(zz, k):
        @pl.loop(0, 4)
        def _(xx):
            GL[k] += nn(GG[zz * 4 + xx, pl.ds(k * T, T)], wrow(1, zz, xx))

    def raw_grad(k):
        rows = pl.ds(k * T, T)
        gl, ln, ls = GL[k], LN[rows], LS[rows]
        gn = gl * glat[...]
        m = jnp.mean(gn * ln, axis=-1, keepdims=True)
        raw = (ls * (gn - ln * m)).astype(BF16)
        RAW[rows] = raw
        MT[k] = jnp.sum(raw.astype(F32) * LAT[rows], axis=-1, keepdims=True) * (1.0 / D)
        LGP[0] += jnp.broadcast_to(jnp.sum(gl * ln, axis=0, keepdims=True), (8, R))

    def back_row(k, zz, xx):
        c = zz * 4 + xx
        grad_in = nt(RAW[pl.ds(k * T, T)], wrow(0, zz, xx)) * gain(c)
        sc = SC[k]
        in_norm = X[k, c].astype(F32) * sc
        g = GG[c, pl.ds(k * T, T)].astype(F32)
        return (g + sc * (grad_in - in_norm * MT[k])).astype(BF16)

    def act_copy(c):
        return remote(R0.at[c], A1.at[c], asend.at[c], arecv.at[c], up_dev)

    def back_copy(c):
        return remote(B0.at[c], GG.at[c, pl.ds(T, T)], bsend.at[c], brecv.at[c], down_dev)

    def result_half(zz):
        @pl.loop(0, 4)
        def _(xx):
            c = zz * 4 + xx
            R0[c] = (X[1, c].astype(F32) + nt(LO[pl.ds(T, T)], wrow(1, zz, xx))).astype(BF16)

            @pl.when(not_last)
            def _():
                act_copy(c).start()

    def send_back_half(zz):
        def body(k, zz, xx):
            c = zz * 4 + xx
            B0[c] = back_row(0, zz, xx)

            @pl.when(not_first)
            def _():
                back_copy(c).start()

        in_order(zz, body)

    OFF = (2, 1, 3, 0)
    POS, NEG = (0, 3), (1, 2)

    def greg(m, zz, h, i1, i2, r0=0, nr=HALF):
        rows = pl.ds(HALF * h + r0, nr)
        return G.at[m, zz, i1, i2, rows] if h == 0 else G.at[m, zz, i2, i1, rows]

    def r_ctx(m, w, h):
        zz = other if w == 0 else zh
        a1, o1, a2, o2 = (0, x, 1, y) if h == 0 else (1, y, 0, x)
        g = functools.partial(greg, m, zz, h)
        return g, a1, o1, a2, [(o2 + k) % 4 for k in OFF], (m * 2 + w) * 2 + h

    def rmsg(m, w, h, i):
        g, a1, o1, a2, j, q = r_ctx(m, w, h)
        u = i % 4
        if i < 4:
            src, land, axis, k = g((o1 + 2) % 4, j[u]), land_a.at[q, u], a1, 1 if u in POS else 3
        elif i < 8:
            src, land, axis, k = g((o1 + 1) % 4, j[u]), land_b.at[q, 0, u], a1, 1
        elif i < 12:
            src, land, axis, k = g((o1 + 3) % 4, j[u]), land_b.at[q, 1, u], a1, 3
        elif i == 12 and m == 0:
            src, land, axis, k = g(o1, j[0]), landu.at[q], a2, 2
        elif i == 12:
            src, land, axis, k = g(o1, j[0], 0, NEAR), landn.at[q], a2, 1
        elif i == 13:
            src, land, axis, k = g(o1, j[0], NEAR, FAR), landf.at[q], a2, 3
        elif i == 14:
            src, land, axis, k = g(o1, j[1]), land1.at[q, 0], a2, 1
        else:
            src, land, axis, k = g(o1, j[2]), land1.at[q, 1], a2, 3
        return remote(src, land, rsend.at[q * 16 + i], rrecv.at[q * 16 + i], along(axis, k))

    def add_into(ref, *lands):
        total = ref[...].astype(F32)
        for land in lands:
            total = total + land[...].astype(F32)
        ref[...] = total.astype(BF16)

    def r_row(m, w, k):
        if k == 0:
            for u in range(4):
                rmsg(m, w, 0, u).start()
        if k == 1:
            for u in NEG:
                rmsg(m, w, 0, 4 + u).start()
        if k == 2:
            for u in POS:
                rmsg(m, w, 0, 8 + u).start()
        rmsg(m, w, 1, k).start()
        rmsg(m, w, 1, (8 if k in POS else 4) + k).start()

    def r_relay(m, w, us=(0, 1, 2, 3)):
        for u in us:
            for h in (0, 1):
                g, a1, o1, a2, j, q = r_ctx(m, w, h)
                rmsg(m, w, h, u).wait_recv()
                add_into(g((o1 + (1 if u in POS else 3)) % 4, j[u]), land_a.at[q, u])
                rmsg(m, w, h, (4 if u in POS else 8) + u).start()

    def r_own(m, w, us):
        for u in us:
            for h in (0, 1):
                g, a1, o1, a2, j, q = r_ctx(m, w, h)
                rmsg(m, w, h, 4 + u).wait_recv()
                rmsg(m, w, h, 8 + u).wait_recv()
                add_into(g(o1, j[u]), land_b.at[q, 0, u], land_b.at[q, 1, u])
                if u == 0:
                    rmsg(m, w, h, 12).start()
                if u == 0 and m == 1:
                    rmsg(m, w, h, 13).start()
                if u in (1, 2) and m == 0:
                    rmsg(m, w, h, 13 + u).start()

    def r_ids(m):
        return [i for i in range(16) if m == 1 or i != 13]

    def r_relay2(m, w):
        for h in (0, 1):
            g, a1, o1, a2, j, q = r_ctx(m, w, h)
            rmsg(m, w, h, 12).wait_recv()
            add_into(g(o1, j[1], 0, NEAR), landn.at[q])
            rmsg(m, w, h, 14).start()
            rmsg(m, w, h, 13).wait_recv()
            add_into(g(o1, j[2], NEAR, FAR), landf.at[q])
            rmsg(m, w, h, 15).start()

    def zgrad(m):
        return remote(G.at[m, other, x, y], landz.at[m], zsend.at[2 + m], zrecv.at[2 + m], partner)

    def r_done(m, w):
        for h in (0, 1):
            g, a1, o1, a2, j, q = r_ctx(m, w, h)
            rmsg(m, w, h, 14).wait_recv()
            rmsg(m, w, h, 15).wait_recv()
            if m == 0:
                rmsg(m, w, h, 12).wait_recv()
            if w == 0:
                far = (landu.at[q],) if m == 0 else ()
                add_into(g(o1, j[3]), land1.at[q, 0], land1.at[q, 1], *far)
        if w == 0:
            zgrad(m).start()
        else:
            zgrad(m).wait_recv()
            out = out_down if m == 0 else out_up
            for h in (0, 1):
                g, a1, o1, a2, j, q = r_ctx(m, w, h)
                rows = pl.ds(HALF * h, HALF)
                total = g(o1, j[3])[...].astype(F32) + landz[m, rows].astype(F32)
                if m == 0:
                    total = total + landu[q].astype(F32)
                out[rows] = total + land1[q, 0].astype(F32) + land1[q, 1].astype(F32)

    def in_order(zz, body):
        @pl.loop(0, 4)
        def _(k):
            body(k, zz, (x + 2 + 3 * k + 3 * (k * (k - 1) // 2)) % 4)

    def after(k, w, m, extra):
        for i in range(4):

            @pl.when(k == i)
            def _():
                r_row(m, w, i)
                for step in extra.get(i, ()):
                    step()

    def up_half(w, extra):
        def body(k, zz, xx):
            c = zz * 4 + xx
            back_copy(c).wait_recv()
            G[1, zz, xx] = tn(GG[c], LO[...]).astype(BF16).reshape(4, UNIT, R)
            after(k, w, 1, extra)
            GL[1] += nn(GG[c, pl.ds(T, T)], wrow(1, zz, xx))

        in_order(other if w == 0 else zh, body)

    def down_half(w, extra):
        def body(k, zz, xx):
            G[0, zz, xx] = nn(NT[zz * 4 + xx], RAW[...]).astype(BF16).reshape(4, UNIT, R)
            after(k, w, 0, extra)

        in_order(other if w == 0 else zh, body)

    def transpose_rows():
        @pl.loop(0, ROWS)
        def _(c):
            NT[c] = N[c].T

    def out_copy(src, dst, c, sem):
        return pltpu.make_async_copy(src.at[c], dst.at[:, col(c)], sem)

    def out_back_half(zz):
        @pl.loop(0, 4)
        def _(xx):
            c = zz * 4 + xx
            OB[c] = back_row(1, zz, xx)
            out_copy(OB, out_grad, c, osem.at[1]).start()

    def lmsg(i):
        axis, k = ((1, 1), (1, 2), (1, 3), (0, 1), (0, 2), (0, 3), (None, 0))[i]
        dev = partner if axis is None else along(axis, k)
        stage = 0 if i < 3 else 1 if i < 6 else 2
        return remote(LGP.at[stage], LGL.at[i], lsend.at[i], lrecv.at[i], dev)

    def lg_start():
        for i in (0, 1, 2):
            lmsg(i).start()

    def lg_stage(stage):
        ids = ((0, 1, 2), (3, 4, 5), (6,))[stage]
        total = LGP[stage]
        for i in ids:
            lmsg(i).wait_recv()
            total = total + LGL[i]
        if stage == 2:
            out_lg[...] = total
        else:
            LGP[stage + 1] = total
            for i in ((3, 4, 5), (6,))[stage]:
                lmsg(i).start()

    def next_norms():
        @pl.loop(0, ROWS)
        def _(c):
            act_copy(c).wait_recv()

        norms(lambda c: A1.at[c], lambda: SC.at[0], lambda c: N1.at[c])

    def next_latent():
        GL[0] = jnp.zeros((T, R), F32)
        latent_half(zh, lambda c: N1[c], GL.at[0])
        latent_half(other, lambda c: N1[c], GL.at[0])
        lat1 = GL[0]
        LO1[...] = (
            lat1 * lax.rsqrt(jnp.mean(lat1 * lat1, axis=-1, keepdims=True) + EPS) * glat[...]
        ).astype(BF16)

    def next_result():
        @pl.loop(0, ROWS)
        def _(c):
            OA[c] = (A1[c].astype(F32) + nt(LO1[...], wrow(1, c // 4, c % 4))).astype(BF16)
            out_copy(OA, out_act, c, osem.at[0]).start()

    def z_start():
        for m in (0, 1):
            zcopy(m).start()

    z_start()
    g_start(0, 0)
    g_start(1, 0)
    LAT[...] = jnp.zeros_like(LAT)
    GL[...] = jnp.zeros_like(GL)
    LGP[0] = jnp.zeros((8, R), F32)
    pltpu.make_async_copy(X.at[0], X.at[0], isem.at[2]).wait()
    norms(lambda c: X.at[0, c], lambda: SC.at[0], lambda c: N.at[c, pl.ds(0, T)])
    g_first(0, 0)
    g_first(1, 0)
    g_second(0, 0, (0,))
    g_second(1, 0, (0,))
    pltpu.make_async_copy(X.at[1], X.at[1], isem.at[3]).wait()
    norms(lambda c: X.at[1, c], lambda: SC.at[1], lambda c: N.at[c, pl.ds(T, T)])
    g_second(0, 0, (1, 2, 3))
    g_second(1, 0, (1, 2, 3))
    zwait(0)
    g_start(0, 1)
    zwait(1)
    g_start(1, 1)
    g_first(0, 1)
    g_first(1, 1)
    transpose_rows()
    g_done(0, 0)
    latent_half(zh, lambda c: N[c], LAT)
    g_second(0, 1)
    g_done(1, 0)
    first_half = GG.at[:, pl.ds(0, T)]
    pltpu.make_async_copy(first_half, first_half, isem.at[4]).wait()
    grad_lat_half(zh, 0)
    g_second(1, 1)
    g_done(0, 1)
    latent_half(other, lambda c: N[c], LAT)
    lat = LAT[...]
    lat_scale = lax.rsqrt(jnp.mean(lat * lat, axis=-1, keepdims=True) + EPS)
    LS[...] = lat_scale
    LN[...] = lat * lat_scale
    LO[...] = (lat * lat_scale * glat[...]).astype(BF16)
    result_half(zh)
    g_done(1, 1)
    grad_lat_half(other, 0)
    raw_grad(0)
    send_back_half(other)
    send_back_half(zh)
    result_half(other)

    def do(f, *args):
        return lambda: f(*args)

    @pl.when(core == 0)
    def _():
        up_half(0, {})
        up_half(1, {})
        r_relay(1, 0)
        raw_grad(1)
        lg_start()
        down_half(0, {})
        r_relay(1, 1)
        r_own(1, 0, (0, 1, 2))
        down_half(1, {})
        r_relay2(1, 0)
        r_relay(0, 0)
        r_own(1, 1, (0, 1, 2))
        r_own(1, 0, (3,))
        r_relay(0, 1)
        r_relay2(1, 1)
        r_done(1, 0)
        r_own(0, 0, (0, 1, 2))
        lg_stage(0)
        r_own(1, 1, (3,))
        r_own(0, 1, (0, 1, 2))
        r_own(0, 0, (3,))
        r_done(0, 0)
        lg_stage(1)
        out_back_half(other)
        r_done(1, 1)
        r_own(0, 1, (3,))
        out_back_half(zh)
        next_norms()
        next_latent()
        next_result()
        lg_stage(2)
        r_done(0, 1)

    @pl.when(core == 1)
    def _():
        up_half(0, {})
        next_norms()
        next_latent()
        next_result()
        up_half(1, {
            0: [do(r_relay, 1, 0)],
            1: [do(r_own, 1, 0, (0, 1))],
            2: [do(r_own, 1, 0, (2,)), do(r_relay2, 1, 0)],
            3: [do(r_own, 1, 0, (3,))],
        })
        raw_grad(1)
        lg_start()
        down_half(0, {})
        r_relay(1, 1)
        down_half(1, {})
        r_done(1, 0)
        r_relay(0, 0)
        r_own(1, 1, (0, 1, 2))
        r_own(0, 0, (0, 1, 2))
        r_relay(0, 1)
        r_relay2(1, 1)
        r_own(0, 0, (3,))
        r_done(0, 0)
        lg_stage(0)
        r_own(0, 1, (0, 1, 2))
        r_own(1, 1, (3,))
        out_back_half(other)
        lg_stage(1)
        r_own(0, 1, (3,))
        r_done(1, 1)
        out_back_half(zh)
        lg_stage(2)
        r_done(0, 1)

    for m in (0, 1):
        zcopy(m).wait_send()
        zgrad(m).wait_send()
        for w in (0, 1):
            for h in (0, 1):
                for i in range(15):
                    gmsg(m, w, h, i).wait_send()
                for i in r_ids(m):
                    rmsg(m, w, h, i).wait_send()
    for i in range(7):
        lmsg(i).wait_send()

    @pl.when(not_last)
    def _():
        @pl.loop(0, ROWS)
        def _(c):
            act_copy(c).wait_send()

    @pl.when(not_first)
    def _():
        @pl.loop(0, ROWS)
        def _(c):
            back_copy(c).wait_send()

    pltpu.make_async_copy(OA, OA, osem.at[0]).wait()
    pltpu.make_async_copy(OB, OB, osem.at[1]).wait()


def finish(acts, grads, down, up, lg, wd, gain, o_acts, o_grads, o_down, o_up, o_gin, o_glat, pad):
    d = lax.axis_index("dp")
    o_acts[...] = acts[...]
    o_grads[...] = grads[...]

    @pl.when(pl.program_id(0) == 0)
    def _():
        o_down[...] = down[...]
        o_up[...] = up[...]
        pad[pl.ds(0, UNIT)] = down[...] * wd[...].astype(F32)
        pad[pl.ds(UNIT, R - UNIT)] = jnp.zeros((R - UNIT, R), F32)
        sums = jnp.sum(pad[...].T, axis=0, keepdims=True)
        first = d * UNIT
        start = pl.multiple_of(jnp.minimum(first // 128 * 128, D - 384), 128)
        window = jnp.broadcast_to(gain[:, pl.ds(start, 384)], (8, 384))
        own = pltpu.roll(window, (384 - (first - start)) % 384, 1)
        o_gin[...] = sums[:, :UNIT] / own[0:1, :UNIT]
        o_glat[...] = pltpu.roll(lg[...], (R - 8 * d) % R, 1)[0:1, :8]


def on_device(
    inflow, entering, arrive_grad, enter_grad, stashed, w_down, w_up, norm_gain, latent_gain
):
    anyspace = pl.BlockSpec(memory_space=pl.ANY)
    vmem = pl.BlockSpec(memory_space=pltpu.VMEM)
    block = pl.BlockSpec((T // 4, D), lambda i: (i, 0))
    rows = (ROWS, T, ROW)
    dma = pltpu.SemaphoreType.DMA
    acts, grads, down, up, lg = pl.pallas_call(
        kernel,
        out_shape=(
            jax.ShapeDtypeStruct((T, D), BF16),
            jax.ShapeDtypeStruct((T, D), BF16),
            jax.ShapeDtypeStruct((UNIT, R), F32),
            jax.ShapeDtypeStruct((UNIT, R), F32),
            jax.ShapeDtypeStruct((8, R), F32),
        ),
        in_specs=[anyspace] * 7 + [vmem] * 2,
        out_specs=(anyspace, anyspace, vmem, vmem, vmem),
        scratch_shapes=[
            pltpu.VMEM((2, 2, 4, 4, UNIT, R), BF16),
            pltpu.VMEM((2, 2, 4, 4, UNIT, R), BF16),
            pltpu.VMEM((2,) + rows, BF16),
            pltpu.VMEM((ROWS, 2 * T, ROW), BF16),
            pltpu.VMEM((ROWS, ROW, 2 * T), BF16),
            pltpu.VMEM((ROWS, 2 * T, ROW), BF16),
            pltpu.VMEM(rows, BF16),
            pltpu.VMEM(rows, BF16),
            pltpu.VMEM(rows, BF16),
            pltpu.VMEM(rows, BF16),
            pltpu.VMEM(rows, BF16),
            pltpu.VMEM(rows, BF16),
            pltpu.VMEM((8, 4, HALF, R), BF16),
            pltpu.VMEM((8, 2, 4, HALF, R), BF16),
            pltpu.VMEM((8, NEAR, R), BF16),
            pltpu.VMEM((8, FAR, R), BF16),
            pltpu.VMEM((4, HALF, R), BF16),
            pltpu.VMEM((8, 2, HALF, R), BF16),
            pltpu.VMEM((2, UNIT, R), BF16),
            pltpu.VMEM((2 * T, R), F32),
            pltpu.VMEM((2 * T, R), F32),
            pltpu.VMEM((2 * T, 1), F32),
            pltpu.VMEM((2 * T, R), BF16),
            pltpu.VMEM((T, R), BF16),
            pltpu.VMEM((2, T, R), F32),
            pltpu.VMEM((2 * T, R), BF16),
            pltpu.VMEM((2, T, 1), F32),
            pltpu.VMEM((2, T, 1), F32),
            pltpu.VMEM((3, 8, R), F32),
            pltpu.VMEM((7, 8, R), F32),
            dma((120,)), dma((120,)),
            dma((4,)), dma((4,)),
            dma((128,)), dma((128,)),
            dma((ROWS,)), dma((ROWS,)),
            dma((ROWS,)), dma((ROWS,)),
            dma((7,)), dma((7,)),
            dma((5,)), dma((2,)),
        ],
        compiler_params=pltpu.CompilerParams(
            collective_id=0, has_side_effects=True, vmem_limit_bytes=60 * 1024 * 1024
        ),
        name="relay",
    )(
        inflow[0], entering[0], arrive_grad[0], enter_grad[0], stashed[0],
        w_down[0], w_up[0].T, norm_gain, latent_gain,
    )
    outs = pl.pallas_call(
        finish,
        out_shape=(
            jax.ShapeDtypeStruct((T, D), BF16),
            jax.ShapeDtypeStruct((T, D), BF16),
            jax.ShapeDtypeStruct((UNIT, R), F32),
            jax.ShapeDtypeStruct((UNIT, R), F32),
            jax.ShapeDtypeStruct((1, UNIT), F32),
            jax.ShapeDtypeStruct((1, 8), F32),
        ),
        grid=(4,),
        in_specs=[block, block] + [vmem] * 5,
        out_specs=(block, block) + (vmem,) * 4,
        scratch_shapes=[pltpu.VMEM((R, R), F32)],
        name="finish",
    )(acts, grads, down, up, lg, w_down[0], norm_gain)
    acts, grads, down, up, gin, glat = outs
    return acts[None], grads[None], down[None], up.T[None], gin, glat


def solution(mesh):
    in_specs = (
        P("section", "dp", None),
        P(None, "dp", None),
        P("section", "dp", None),
        P(None, "dp", None),
        P("section", "dp", None),
        P("section", "dp", None),
        P("section", None, "dp"),
        P("section", None),
        P("section", None),
    )
    out_specs = (
        P("section", "dp", None),
        P("section", "dp", None),
        P("section", "dp", None),
        P("section", None, "dp"),
        P("section", "dp"),
        P("section", "dp"),
    )
    return jax.shard_map(
        on_device, mesh=mesh, in_specs=in_specs, out_specs=out_specs, check_vma=False
    )
```

time: 237 us -> 117 us (0.49)
  the two profiles are of different devices: /device:TPU:32 before, /device:TPU:1 now
where the time goes in v3:
time: 117 us
  Pallas kernels  116 us (99%)
    pallas_call x1, Pallas kernels, on_device(): pl.pallas_call(kernel, out_shape=(jax.ShapeDtypeStruct((T, D), BF16), jax...  111 us
    pallas_call x1, Pallas kernels, on_device(): pl.pallas_call(finish, out_shape=(jax.ShapeDtypeStruct((T, D), BF16), jax...  4.89 us

profile of v3, /device:TPU:1, one launch (start us, length us, event | category | flops | bytes accessed | tf_op | source)
XLA Modules:
  0.0 117.1 jit_solution(6362256592321015068)
XLA Ops:
  0.6 111.4 %relay.1 = (bf16[128,7168]{1,0:T(8,128)(2,1)}, bf16[128,7168]{1,0:T(8,128)(2,1)}, f32[224,256]{1,0:T(8,128)}, f32[224,256]{1,0:T(8,128)}, f32[8,256]{1,0:T(8,128)}) custom-call(bf16[128,7168]{1,0:T(8,128)(2,1)} %bitcast.15, bf16[128,7168]{1,0:T(8,128)(2,1)} %bitcast.16, bf16[128,7168]{1,0:T(8,128)(2,1)} %bitcast.17, bf16[128,7168]{1,0:T(8,128)(2,1)} %bitcast.18, ...), custom_call_target="tpu_custom_call" | custom-call | tf_op jit(solution)/shard_map/relay/pallas_call | solution.py:628
  112.1 4.9 %finish.1 = (bf16[128,7168]{1,0:T(8,128)(2,1)}, bf16[128,7168]{1,0:T(8,128)(2,1)}, f32[224,256]{1,0:T(8,128)}, f32[224,256]{1,0:T(8,128)}, f32[1,224]{1,0:T(1,128)}, /*index=5*/f32[1,8]{1,0:T(1,128)}) custom-call(bf16[128,7168]{1,0:T(8,128)(2,1)} %get-tuple-element.17.acts, bf16[128,7168]{1,0:T(8,128)(2,1)} %get-tuple-element.18.grads, ...), custom_call_target="tpu_custom_call" | custom-call | tf_op jit(solution)/shard_map/finish/pallas_call | solution.py:686

commit v4 on v3

--- a/solution.py
+++ b/solution.py
@@ -42,7 +42,7 @@
     land_a, land_b, landn, landf, landu, land1, landz,
     LAT, LN, LS, LO, LO1, GL, RAW, MT, SC, LGP, LGL,
     gsend, grecv, zsend, zrecv, rsend, rrecv, asend, arecv, bsend, brecv,
-    lsend, lrecv, isem, osem,
+    lsend, lrecv, isem, osem, go,
 ):
     s = lax.axis_index("section")
     d = lax.axis_index("dp")
@@ -71,6 +71,12 @@
             src_ref=src, dst_ref=dst, send_sem=ssem, recv_sem=rsem, device_id=dev, device_id_type=MESH
         )
 
+    barrier = pltpu.get_barrier_semaphore()
+    peers = [along(ax, k) for ax in (0, 1) for k in (1, 2, 3)] + [partner]
+    peers += [((s + 1) % 8, d), ((s + 7) % 8, d)]
+    for dev in peers:
+        pl.semaphore_signal(barrier, inc=1, device_id=dev, device_id_type=MESH)
+
     wcopy = [
         pltpu.make_async_copy(ref, W.at[m, zh, x, y], isem.at[m]) for m, ref in enumerate((wd_in, wu_in))
     ]
@@ -89,11 +95,6 @@
     load_start(inflow, lambda c: X.at[1, c], isem.at[3])
     load_start(arrive, lambda c: GG.at[c, pl.ds(0, T)], isem.at[4])
 
-    barrier = pltpu.get_barrier_semaphore()
-    peers = [along(ax, k) for ax in (0, 1) for k in (1, 2, 3)] + [partner]
-    peers += [((s + 1) % 8, d), ((s + 7) % 8, d)]
-    for dev in peers:
-        pl.semaphore_signal(barrier, inc=1, device_id=dev, device_id_type=MESH)
     pl.semaphore_wait(barrier, len(peers))
 
     @pl.when(s == 0)
@@ -301,7 +302,7 @@
                 add_into(g((o1 + (1 if u in POS else 3)) % 4, j[u]), land_a.at[q, u])
                 rmsg(m, w, h, (4 if u in POS else 8) + u).start()
 
-    def r_own(m, w, us):
+    def r_own(m, w, us=(0, 1, 2, 3)):
         for u in us:
             for h in (0, 1):
                 g, a1, o1, a2, j, q = r_ctx(m, w, h)
@@ -445,6 +446,24 @@
             OA[c] = (A1[c].astype(F32) + nt(LO1[...], wrow(1, c // 4, c % 4))).astype(BF16)
             out_copy(OA, out_act, c, osem.at[0]).start()
 
+    def g_sent():
+        for m in (0, 1):
+            zcopy(m).wait_send()
+            for w in (0, 1):
+                for h in (0, 1):
+                    for i in range(15):
+                        gmsg(m, w, h, i).wait_send()
+
+    def r_sent(m):
+        for w in (0, 1):
+            for h in (0, 1):
+                for i in r_ids(m):
+                    rmsg(m, w, h, i).wait_send()
+
+    def up_sent():
+        zgrad(1).wait_send()
+        r_sent(1)
+
     def z_start():
         for m in (0, 1):
             zcopy(m).start()
@@ -468,13 +487,30 @@
     zwait(0)
     g_start(0, 1)
     zwait(1)
-    g_start(1, 1)
-    g_first(0, 1)
-    g_first(1, 1)
-    transpose_rows()
+
+    @pl.when(core == 0)
+    def _():
+        g_start(1, 1)
+        g_first(0, 1)
+        g_first(1, 1)
+        pl.semaphore_signal(go, inc=1, device_id=up_dev, device_id_type=MESH)
+
+    @pl.when(core == 1)
+    def _():
+        g_first(0, 1)
+        g_second(0, 1)
+        transpose_rows()
+        pl.semaphore_wait(go, 1)
+        g_start(1, 1)
+        g_first(1, 1)
+
+    @pl.when(core == 0)
+    def _():
+        transpose_rows()
+        g_second(0, 1)
+
     g_done(0, 0)
     latent_half(zh, lambda c: N[c], LAT)
-    g_second(0, 1)
     g_done(1, 0)
     first_half = GG.at[:, pl.ds(0, T)]
     pltpu.make_async_copy(first_half, first_half, isem.at[4]).wait()
@@ -493,7 +529,6 @@
     raw_grad(0)
     send_back_half(other)
     send_back_half(zh)
-    result_half(other)
 
     def do(f, *args):
         return lambda: f(*args)
@@ -502,6 +537,7 @@
     def _():
         up_half(0, {})
         up_half(1, {})
+        result_half(other)
         r_relay(1, 0)
         raw_grad(1)
         lg_start()
@@ -527,6 +563,8 @@
         r_done(1, 1)
         r_own(0, 1, (3,))
         out_back_half(zh)
+        g_sent()
+        up_sent()
         next_norms()
         next_latent()
         next_result()
@@ -535,10 +573,12 @@
 
     @pl.when(core == 1)
     def _():
+        result_half(other)
         up_half(0, {})
         next_norms()
         next_latent()
         next_result()
+        g_sent()
         up_half(1, {
             0: [do(r_relay, 1, 0)],
             1: [do(r_own, 1, 0, (0, 1))],
@@ -553,31 +593,23 @@
         r_done(1, 0)
         r_relay(0, 0)
         r_own(1, 1, (0, 1, 2))
-        r_own(0, 0, (0, 1, 2))
         r_relay(0, 1)
+        r_own(0, 0)
         r_relay2(1, 1)
-        r_own(0, 0, (3,))
         r_done(0, 0)
         lg_stage(0)
-        r_own(0, 1, (0, 1, 2))
+        r_own(0, 1)
         r_own(1, 1, (3,))
+        lg_stage(1)
         out_back_half(other)
-        lg_stage(1)
-        r_own(0, 1, (3,))
         r_done(1, 1)
         out_back_half(zh)
+        up_sent()
         lg_stage(2)
         r_done(0, 1)
 
-    for m in (0, 1):
-        zcopy(m).wait_send()
-        zgrad(m).wait_send()
-        for w in (0, 1):
-            for h in (0, 1):
-                for i in range(15):
-                    gmsg(m, w, h, i).wait_send()
-                for i in r_ids(m):
-                    rmsg(m, w, h, i).wait_send()
+    zgrad(0).wait_send()
+    r_sent(0)
     for i in range(7):
         lmsg(i).wait_send()
 
@@ -622,7 +654,7 @@
 ):
     anyspace = pl.BlockSpec(memory_space=pl.ANY)
     vmem = pl.BlockSpec(memory_space=pltpu.VMEM)
-    block = pl.BlockSpec((T // 4, D), lambda i: (i, 0))
+    block = pl.BlockSpec((T // 2, D), lambda i: (i, 0))
     rows = (ROWS, T, ROW)
     dma = pltpu.SemaphoreType.DMA
     acts, grads, down, up, lg = pl.pallas_call(
@@ -674,6 +706,7 @@
             dma((ROWS,)), dma((ROWS,)),
             dma((7,)), dma((7,)),
             dma((5,)), dma((2,)),
+            pltpu.SemaphoreType.REGULAR,
         ],
         compiler_params=pltpu.CompilerParams(
             collective_id=0, has_side_effects=True, vmem_limit_bytes=60 * 1024 * 1024
@@ -693,7 +726,7 @@
             jax.ShapeDtypeStruct((1, UNIT), F32),
             jax.ShapeDtypeStruct((1, 8), F32),
         ),
-        grid=(4,),
+        grid=(2,),
         in_specs=[block, block] + [vmem] * 5,
         out_specs=(block, block) + (vmem,) * 4,
         scratch_shapes=[pltpu.VMEM((R, R), F32)],

time: 117 us -> 115 us (0.983)
  Pallas kernels: 116 us -> 114 us
    pallas_call x1, Pallas kernels: 111 us -> 110 us  [on_device(): pl.pallas_call(kernel, out_shape=(jax.ShapeDtypeStruct((T, D), BF16), jax...]
where the time goes in v4:
time: 115 us
  Pallas kernels  114 us (99%)
    pallas_call x1, Pallas kernels, on_device(): pl.pallas_call(kernel, out_shape=(jax.ShapeDtypeStruct((T, D), BF16), jax...  110 us
    pallas_call x1, Pallas kernels, on_device(): pl.pallas_call(finish, out_shape=(jax.ShapeDtypeStruct((T, D), BF16), jax...  3.9 us

profile of v4, /device:TPU:1, one launch (start us, length us, event | category | flops | bytes accessed | tf_op | source)
XLA Modules:
  0.0 114.9 jit_solution(9537531807671721610)
XLA Ops:
  0.6 110.2 %relay.1 = (bf16[128,7168]{1,0:T(8,128)(2,1)}, bf16[128,7168]{1,0:T(8,128)(2,1)}, f32[224,256]{1,0:T(8,128)}, f32[224,256]{1,0:T(8,128)}, f32[8,256]{1,0:T(8,128)}) custom-call(bf16[128,7168]{1,0:T(8,128)(2,1)} %bitcast.15, bf16[128,7168]{1,0:T(8,128)(2,1)} %bitcast.16, bf16[128,7168]{1,0:T(8,128)(2,1)} %bitcast.17, bf16[128,7168]{1,0:T(8,128)(2,1)} %bitcast.18, ...), custom_call_target="tpu_custom_call" | custom-call | tf_op jit(solution)/shard_map/relay/pallas_call | solution.py:660
  110.9 3.9 %finish.1 = (bf16[128,7168]{1,0:T(8,128)(2,1)}, bf16[128,7168]{1,0:T(8,128)(2,1)}, f32[224,256]{1,0:T(8,128)}, f32[224,256]{1,0:T(8,128)}, f32[1,224]{1,0:T(1,128)}, /*index=5*/f32[1,8]{1,0:T(1,128)}) custom-call(bf16[128,7168]{1,0:T(8,128)(2,1)} %get-tuple-element.17.acts, bf16[128,7168]{1,0:T(8,128)(2,1)} %get-tuple-element.18.grads, ...), custom_call_target="tpu_custom_call" | custom-call | tf_op jit(solution)/shard_map/finish/pallas_call | solution.py:719
